TPU v7x, 32 devices: a whole 2x2x4 slice. The times are simulated.
32 devices in a mesh: dp: 8 (over y, x, core), fsdp: 4 (over z).
Axes of the slice: x: 2, y: 2, z: 4, core: 2. Of those that a mesh axis runs over, the one named last changes fastest.
Arguments:
- single: bfloat16 [96, 384, 768], P(('dp', 'fsdp')), may hold values from -6 to 6
- condition: bfloat16 [96, 384, 384], P(('dp', 'fsdp')), may hold values from -6 to 6
- pair_tensor: bfloat16 [2, 384, 384, 128], P(None, 'dp', 'fsdp'), may hold values from -6 to 6
- counts: int32 [2], replicated, may hold values from 96 to 384, as said below
- complex_of: int32 [96], P(('dp', 'fsdp')), may hold values from 0 to 1
- cotangent: bfloat16 [96, 384, 768], P(('dp', 'fsdp')), may hold values from -6 to 6
- condition_gain: bfloat16 [384], P('fsdp'), may hold values from 0.099609375 to 1.8984375
- scale_weight: bfloat16 [384, 768], P('fsdp'), may hold values from -0.3125 to 0.3125
- scale_bias: bfloat16 [768], P('fsdp'), may hold values from -4 to 4
- shift_weight: bfloat16 [384, 768], P('fsdp'), may hold values from -0.3125 to 0.3125
- query_weight: bfloat16 [768, 768], P('fsdp'), may hold values from -0.3125 to 0.3125
- query_bias: bfloat16 [768], P('fsdp'), may hold values from -3 to 3
- key_weight: bfloat16 [768, 768], P('fsdp'), may hold values from -0.3125 to 0.3125
- value_weight: bfloat16 [768, 768], P('fsdp'), may hold values from -0.21875 to 0.21875
- gate_weight: bfloat16 [768, 768], P('fsdp'), may hold values from -0.21875 to 0.21875
- output_weight: bfloat16 [768, 768], P('fsdp'), may hold values from -2.5 to 2.5
- pair_gain: bfloat16 [128], P('fsdp'), may hold values from 0.099609375 to 1.8984375
- pair_weight: bfloat16 [128, 16], P('fsdp'), may hold values from -0.5 to 0.5
- branch_gate_weight: bfloat16 [384, 768], P('fsdp'), may hold values from -0.3125 to 0.3125
- branch_gate_bias: bfloat16 [768], P('fsdp'), may hold values from -4 to 4
- transition_gain: bfloat16 [384], P('fsdp'), may hold values from 0.099609375 to 1.8984375
- transition_scale_weight: bfloat16 [384, 768], P('fsdp'), may hold values from -0.3125 to 0.3125
- transition_scale_bias: bfloat16 [768], P('fsdp'), may hold values from -4 to 4
- transition_shift_weight: bfloat16 [384, 768], P('fsdp'), may hold values from -0.3125 to 0.3125
- hidden_gate: bfloat16 [768, 1536], P('fsdp'), may hold values from -0.21875 to 0.21875
- hidden_value: bfloat16 [768, 1536], P('fsdp'), may hold values from -0.21875 to 0.21875
- hidden_output: bfloat16 [1536, 768], P('fsdp'), may hold values from -0.3125 to 0.3125
- final_gate_weight: bfloat16 [384, 768], P('fsdp'), may hold values from -0.3125 to 0.3125
- final_gate_bias: bfloat16 [768], P('fsdp'), may hold values from -4 to 4
Outputs:
- output: bfloat16 [96, 384, 768], P(('dp', 'fsdp'))
- single_grad: float32 [96, 384, 768], P(('dp', 'fsdp'))
- condition_grad: float32 [96, 384, 384], P(('dp', 'fsdp'))
- pair_grad: float32 [2, 384, 384, 128], P(None, 'dp', 'fsdp')
- condition_gain_grad: float32 [384], P('fsdp')
- scale_weight_grad: float32 [384, 768], P('fsdp')
- scale_bias_grad: float32 [768], P('fsdp')
- shift_weight_grad: float32 [384, 768], P('fsdp')
- query_weight_grad: float32 [768, 768], P('fsdp')
- query_bias_grad: float32 [768], P('fsdp')
- key_weight_grad: float32 [768, 768], P('fsdp')
- value_weight_grad: float32 [768, 768], P('fsdp')
- gate_weight_grad: float32 [768, 768], P('fsdp')
- output_weight_grad: float32 [768, 768], P('fsdp')
- pair_gain_grad: float32 [128], P('fsdp')
- pair_weight_grad: float32 [128, 16], P('fsdp')
- branch_gate_weight_grad: float32 [384, 768], P('fsdp')
- branch_gate_bias_grad: float32 [768], P('fsdp')
- transition_gain_grad: float32 [384], P('fsdp')
- transition_scale_weight_grad: float32 [384, 768], P('fsdp')
- transition_scale_bias_grad: float32 [768], P('fsdp')
- transition_shift_weight_grad: float32 [384, 768], P('fsdp')
- hidden_gate_grad: float32 [768, 1536], P('fsdp')
- hidden_value_grad: float32 [768, 1536], P('fsdp')
- hidden_output_grad: float32 [1536, 768], P('fsdp')
- final_gate_weight_grad: float32 [384, 768], P('fsdp')
- final_gate_bias_grad: float32 [768], P('fsdp')
Inputs may be any that keep to these rules, and one draw needn't show every extreme that they name: `counts`: token slots at and beyond a complex's count are padding; one complex in each draw has exactly 384 tokens.
All inputs are finite; a program needn't handle non-finite values.
Results may differ from a plain program's by a relative error of at most 0.025.
Values may be sent and summed in bfloat16 or wider, within the bound.
A program may use at most 320 MiB of HBM per device.

v0:
```python
import functools

import jax
import jax.numpy as jnp
from jax import lax
from jax.experimental import pallas as pl
from jax.experimental.pallas import tpu as pltpu
from jax.sharding import PartitionSpec as P

BF = jnp.bfloat16
F32 = jnp.float32
EPSILON = 1e-05
DP = "dp"
FS = "fsdp"
MIB = 1024 * 1024
NEGATIVE = -1000000000.0


def norm(v):
    c = v - jnp.mean(v, axis=-1, keepdims=True)
    r = lax.rsqrt(jnp.mean(c * c, axis=-1, keepdims=True) + EPSILON)
    return c * r, r


def norm_back(n, r, u):
    return r * (u - jnp.mean(u, axis=-1, keepdims=True) - n * jnp.mean(u * n, axis=-1, keepdims=True))


def sig(v):
    return 0.5 * jnp.tanh(0.5 * v) + 0.5


def dot(a, b):
    return jnp.dot(a, b, preferred_element_type=F32)


def dot_nt(a, b):
    return lax.dot_general(a, b, (((1,), (1,)), ((), ())), preferred_element_type=F32)


def dot_tn(a, b):
    return lax.dot_general(a, b, (((0,), (0,)), ((), ())), preferred_element_type=F32)


def flat(ref):
    v = ref[...]
    return v.reshape(v.shape[0] * v.shape[1], v.shape[2])


def colsum(v):
    return jnp.sum(v.astype(F32), axis=0, keepdims=True)


def first_kernel(x, c, wq, wk, wv, wg, ws, wh, sm, fi, q, k, v, gp, sp, cl):
    cn, _ = norm(c[...].astype(F32))
    low = (cn * sm[5:6, : cn.shape[1]]).astype(BF)
    cl[...] = low
    pre = dot(low, flat(ws)) + sm[0:1, :]
    shift = dot(low, flat(wh))
    sp[...] = pre.astype(BF)
    an, _ = norm(x[...].astype(F32))
    first = (sig(pre) * an + shift).astype(BF)
    fi[...] = first
    q[...] = (dot(first, flat(wq)) + sm[1:2, :]).astype(BF)
    k[...] = dot(first, flat(wk)).astype(BF)
    v[...] = dot(first, flat(wv)).astype(BF)
    gp[...] = dot(first, flat(wg)).astype(BF)


def whole(shape):
    return pl.BlockSpec(shape, lambda *i: (0,) * len(shape), pipeline_mode=pl.Buffered(1))


def part(z, rows, width, at):
    return pl.BlockSpec((z, rows, width), lambda *i: (0, at, 0), pipeline_mode=pl.Buffered(1))


def rows_of(tb, width):
    return pl.BlockSpec((tb, width), lambda i, *_: (i, 0))


def params(limit, **kw):
    return pltpu.CompilerParams(vmem_limit_bytes=limit * MIB, **kw)


def cost(flops, nbytes, trans=0):
    return pl.CostEstimate(flops=int(flops), bytes_accessed=int(nbytes), transcendentals=int(trans))


def run_first(x, c, g1, sm, tb):
    t, d = x.shape
    dc = c.shape[1]
    z = g1.shape[0]
    dz, cz = d // z, dc // z
    sds = jax.ShapeDtypeStruct
    return pl.pallas_call(
        first_kernel,
        grid=(t // tb,),
        in_specs=[rows_of(tb, d), rows_of(tb, dc)]
        + [part(z, dz, d, i) for i in range(4)]
        + [part(z, cz, d, 4 * dz // cz), part(z, cz, d, 4 * dz // cz + 1), whole(sm.shape)],
        out_specs=[rows_of(tb, d)] * 6 + [rows_of(tb, dc)],
        out_shape=[sds((t, d), BF)] * 6 + [sds((t, dc), BF)],
        compiler_params=params(60),
        cost_estimate=cost(2 * t * d * (4 * d + 2 * dc), 20 * MIB),
        name="first",
    )(x, c, g1, g1, g1, g1, g1, g1, sm)


def windows(per, hs):
    out = []
    for j in range(per):
        lo = j * hs
        w = min(lo // 128 * 128, max(per * hs - 256, 0))
        out.append((w, lo - w))
    return out


def lane_mask(o, hs, width):
    lane = lax.broadcasted_iota(jnp.int32, (1, width), 1)
    return jnp.where((lane >= o) & (lane < o + hs), 1.0, 0.0).astype(BF)


def put(acc, w, width, val):
    for b in range(width // 128):
        key = w // 128 + b
        piece = val[:, 128 * b : 128 * b + 128]
        acc[key] = piece if key not in acc else acc[key] + piece


def attend_kernel(per, hs, comp, cnt, q, k, v, b, gp, p_out, att, gated):
    n = comp[pl.program_id(0)]
    width = min(256, per * hs)
    limit = cnt[n]
    mrow = jnp.where(
        lax.broadcasted_iota(jnp.int32, (1, k.shape[0]), 1) < limit, 0.0, NEGATIVE
    ).astype(F32)
    scale = hs ** (-0.5)
    acc = {}
    for j, (w, o) in enumerate(windows(per, hs)):
        m = lane_mask(o, hs, width)
        s = dot_nt(q[:, w : w + width] * m, k[:, w : w + width]) * scale
        s = s + (b[0, j].astype(F32) + mrow)
        e = jnp.exp(s - jnp.max(s, axis=-1, keepdims=True))
        pb = (e * (1.0 / jnp.sum(e, axis=-1, keepdims=True))).astype(BF)
        p_out[0, j] = pb
        put(acc, w, width, dot(pb, v[:, w : w + width] * m))
    for key, val in acc.items():
        cols = slice(128 * key, 128 * key + 128)
        att[:, cols] = val.astype(BF)
        gated[:, cols] = (sig(gp[:, cols].astype(F32)) * val).astype(BF)


def run_attend(comp, cnt, q, k, v, gp, bias, groups):
    copies = comp.shape[0]
    t, d = q.shape
    rows = t // copies
    heads = bias.shape[1]
    per, dg = heads // groups, d // groups
    blk = pl.BlockSpec((rows, dg), lambda c, g, *_: (c, g))
    sds = jax.ShapeDtypeStruct
    return pl.pallas_call(
        functools.partial(attend_kernel, per, d // heads),
        grid_spec=pltpu.PrefetchScalarGridSpec(
            num_scalar_prefetch=2,
            grid=(copies, groups),
            in_specs=[
                blk,
                blk,
                blk,
                pl.BlockSpec((1, per, rows, rows), lambda c, g, comp, cnt: (comp[c], g, 0, 0)),
                blk,
            ],
            out_specs=[
                pl.BlockSpec((1, per, rows, rows), lambda c, g, *_: (c, g, 0, 0)),
                blk,
                blk,
            ],
        ),
        out_shape=[sds((copies, heads, rows, rows), BF), sds((t, d), BF), sds((t, d), BF)],
        compiler_params=params(60),
        cost_estimate=cost(2 * 2 * t * rows * heads * 256, 40 * MIB, t * rows * heads),
        name="attend",
    )(comp, cnt, q, k, v, bias, gp)


def attend_back_kernel(per, hs, comp, p, q, k, v, da, at, dq, dk, dv, db, acc):
    c = pl.program_id(1)
    last = pl.num_programs(1) - 1
    n = comp[c]
    width = min(256, per * hs)
    scale = hs ** (-0.5)

    @pl.when(c == 0)
    def _():
        acc[...] = jnp.zeros_like(acc)

    aq, ak, av = {}, {}, {}
    prod = da[...].astype(F32) * at[...].astype(F32)
    lane = lax.broadcasted_iota(jnp.int32, (1, per * hs), 1)
    for j, (w, o) in enumerate(windows(per, hs)):
        m = lane_mask(o, hs, width)
        lo = w + o
        inside = (lane >= lo) & (lane < lo + hs)
        delta = jnp.sum(jnp.where(inside, prod, 0.0), axis=-1, keepdims=True)
        pj = p[0, j]
        win = slice(w, w + width)
        dam = da[:, win] * m
        dp = dot_nt(dam, v[:, win])
        ds = pj.astype(F32) * (dp - delta)
        acc[n, j] += ds
        dsb = ds.astype(BF)
        put(av, w, width, dot_tn(pj, dam))
        put(aq, w, width, dot(dsb, k[:, win] * m))
        put(ak, w, width, dot_tn(dsb, q[:, win] * m))
    for key in aq:
        cols = slice(128 * key, 128 * key + 128)
        dq[:, cols] = (aq[key] * scale).astype(BF)
        dk[:, cols] = (ak[key] * scale).astype(BF)
        dv[:, cols] = av[key].astype(BF)

    @pl.when(c == last)
    def _():
        db[...] = acc[...].astype(BF)


def run_attend_back(comp, p, q, k, v, da, att, ncomp, groups):
    copies, heads, rows, _ = p.shape
    t, d = q.shape
    per, dg = heads // groups, d // groups
    blk = pl.BlockSpec((rows, dg), lambda g, c, *_: (c, g))
    sds = jax.ShapeDtypeStruct
    return pl.pallas_call(
        functools.partial(attend_back_kernel, per, d // heads),
        grid_spec=pltpu.PrefetchScalarGridSpec(
            num_scalar_prefetch=1,
            grid=(groups, copies),
            in_specs=[pl.BlockSpec((1, per, rows, rows), lambda g, c, *_: (c, g, 0, 0))]
            + [blk] * 5,
            out_specs=[blk] * 3
            + [
                pl.BlockSpec(
                    (ncomp, per, rows, rows),
                    lambda g, c, *_: (0, g, 0, 0),
                    pipeline_mode=pl.Buffered(1),
                )
            ],
            scratch_shapes=[pltpu.VMEM((ncomp, per, rows, rows), F32)],
        ),
        out_shape=[sds((t, d), BF)] * 3 + [sds((ncomp, heads, rows, rows), BF)],
        compiler_params=params(60),
        cost_estimate=cost(4 * 2 * t * rows * heads * 256, 40 * MIB),
        name="attend_back",
    )(comp, p, q, k, v, da, att)


def middle_kernel(per_copy, comp, cnt, x, c, ct, gat, att, gp, wo, hl, hr, vl, vr, ho, bg, ts, th, fg, sm,
                  out, gm_o, dc_o, si_o, act_o, cl_o, g2_o, gz2_o, gh_o, gv_o, gsc_o, gsh_o, g1_o, gz1_o, da_o, dg_o, vec):
    i = pl.program_id(0)
    tb, d = x.shape
    dc = c.shape[1]
    copy = i // per_copy
    limit = cnt[comp[copy]] - (i % per_copy) * tb
    keep = jnp.where(lax.broadcasted_iota(jnp.int32, (tb, 1), 0) < limit, 1.0, 0.0).astype(F32)

    low = c[...]
    y1 = dot(gat[...], flat(wo))
    z1 = sig(dot(low, flat(bg)) + sm[2:3, :])
    kz1 = keep * z1
    mid = x[...].astype(F32) + kz1 * y1
    cn, cr = norm(low.astype(F32))
    gain = sm[6:7, :dc]
    cl = (cn * gain).astype(BF)
    cl_o[...] = cl
    s2 = sig(dot(cl, flat(ts)) + sm[3:4, :])
    mn, mr = norm(mid)
    si = (s2 * mn + dot(cl, flat(th))).astype(BF)
    si_o[...] = si
    zh = ho.shape[0] // 2
    kept = []
    y2 = None
    for half, (hg, hv) in enumerate(((hl, vl), (hr, vr))):
        u = dot(si, flat(hg))
        w = dot(si, flat(hv))
        su = sig(u)
        silu = u * su
        act = (silu * w).astype(BF)
        act_o[:, half * d : half * d + d] = act
        kept.append((w * su * (1.0 + u - silu), silu))
        hov = ho[half * zh : half * zh + zh]
        term = dot(act, hov.reshape(d, d))
        y2 = term if y2 is None else y2 + term
    z2 = sig(dot(low, flat(fg)) + sm[4:5, :])
    g = ct[...].astype(F32)
    kz2 = keep * z2
    out[...] = (mid + kz2 * y2).astype(BF)
    gk = g * kz2
    g2 = gk.astype(BF)
    gz2 = (gk * y2 * (1.0 - z2)).astype(BF)
    g2_o[...] = g2
    gz2_o[...] = gz2
    e = None
    for half, (hg, hv) in enumerate(((hl, vl), (hr, vr))):
        hov = ho[half * zh : half * zh + zh]
        ga = dot_nt(g2, hov.reshape(d, d))
        du, silu = kept[half]
        gh = (ga * du).astype(BF)
        gv = (ga * silu).astype(BF)
        gh_o[:, half * d : half * d + d] = gh
        gv_o[:, half * d : half * d + d] = gv
        term = dot_nt(gh, flat(hg)) + dot_nt(gv, flat(hv))
        e = term if e is None else e + term
    t = e * s2
    gsc = (t * mn * (1.0 - s2)).astype(BF)
    gsh = e.astype(BF)
    gsc_o[...] = gsc
    gsh_o[...] = gsh
    gc = dot_nt(gsc, flat(ts)) + dot_nt(gsh, flat(th))
    gm = g + norm_back(mn, mr, t)
    gm_o[...] = gm
    kz = gm * kz1
    g1 = kz.astype(BF)
    gz1 = (kz * y1 * (1.0 - z1)).astype(BF)
    g1_o[...] = g1
    gz1_o[...] = gz1
    dc_o[...] = norm_back(cn, cr, gc * gain) + dot_nt(gz2, flat(fg)) + dot_nt(gz1, flat(bg))
    gg = dot_nt(g1, flat(wo))
    sp = sig(gp[...].astype(F32))
    da = gg * sp
    da_o[...] = da.astype(BF)
    dg_o[...] = (da * att[...].astype(F32) * (1.0 - sp)).astype(BF)

    @pl.when(i == 0)
    def _():
        vec[...] = jnp.zeros_like(vec)

    vec[2:3, :] += colsum(gz1)
    vec[3:4, :] += colsum(gsc)
    vec[4:5, :] += colsum(gz2)
    vec[6:7, :dc] += jnp.sum(gc * cn, axis=0, keepdims=True)


def run_middle(comp, cnt, x, c, ct, gat, att, gp, g2, sm, tb):
    t, d = x.shape
    dc = c.shape[1]
    z = g2.shape[0]
    ff = 2 * d
    dz, cz, fz = d // z, dc // z, ff // z
    sds = jax.ShapeDtypeStruct
    per_copy = t // comp.shape[0] // tb
    w9 = (fz + 5 * dz) // cz
    outs = [
        (d, BF), (d, F32), (dc, F32), (d, BF), (ff, BF), (dc, BF), (d, BF), (d, BF), (ff, BF), (ff, BF),
        (d, BF), (d, BF), (d, BF), (d, BF), (d, BF), (d, BF),
    ]
    return pl.pallas_call(
        functools.partial(middle_kernel, per_copy),
        grid_spec=pltpu.PrefetchScalarGridSpec(
            num_scalar_prefetch=2,
            grid=(t // tb,),
            in_specs=[rows_of(tb, d), rows_of(tb, dc)]
            + [rows_of(tb, d)] * 4
            + [part(z, dz, d, fz // dz + i) for i in range(5)]
            + [part(z, fz, d, 0)]
            + [part(z, cz, d, w9 + i) for i in range(4)]
            + [whole(sm.shape)],
            out_specs=[rows_of(tb, w) for w, _ in outs] + [whole((8, d))],
        ),
        out_shape=[sds((t, w), k) for w, k in outs] + [sds((8, d), F32)],
        compiler_params=params(60),
        cost_estimate=cost(2 * t * (2 * d * d + 8 * d * dc + 6 * d * ff), 60 * MIB),
        name="middle",
    )(comp, cnt, x, c, ct, gat, att, gp, g2, g2, g2, g2, g2, g2, g2, g2, g2, g2, sm)


def last_kernel(dq, dk, dv, dg, x, c, sp, gm, dcp, wq, wk, wv, wg, ws, wh, sm, sg_o, cg_o, gsc_o, gsh_o, vec):
    dc = c.shape[1]
    e = (
        dot_nt(dq[...], flat(wq))
        + dot_nt(dk[...], flat(wk))
        + dot_nt(dv[...], flat(wv))
        + dot_nt(dg[...], flat(wg))
    )
    an, ar = norm(x[...].astype(F32))
    s = sig(sp[...].astype(F32))
    t = e * s
    gsc = (t * an * (1.0 - s)).astype(BF)
    gsh = e.astype(BF)
    gsc_o[...] = gsc
    gsh_o[...] = gsh
    sg_o[...] = gm[...] + norm_back(an, ar, t)
    gc = dot_nt(gsc, flat(ws)) + dot_nt(gsh, flat(wh))
    cn, cr = norm(c[...].astype(F32))
    cg_o[...] = dcp[...] + norm_back(cn, cr, gc * sm[5:6, :dc])

    @pl.when(pl.program_id(0) == 0)
    def _():
        vec[...] = jnp.zeros_like(vec)

    vec[0:1, :] += colsum(gsc)
    vec[1:2, :] += colsum(dq[...])
    vec[5:6, :dc] += jnp.sum(gc * cn, axis=0, keepdims=True)


def run_last(dq, dk, dv, dg, x, c, sp, gm, dcp, g1, sm, tb):
    t, d = x.shape
    dc = c.shape[1]
    z = g1.shape[0]
    dz, cz = d // z, dc // z
    sds = jax.ShapeDtypeStruct
    return pl.pallas_call(
        last_kernel,
        grid=(t // tb,),
        in_specs=[rows_of(tb, d)] * 5
        + [rows_of(tb, dc), rows_of(tb, d), rows_of(tb, d), rows_of(tb, dc)]
        + [part(z, dz, d, i) for i in range(4)]
        + [part(z, cz, d, 4 * dz // cz), part(z, cz, d, 4 * dz // cz + 1), whole(sm.shape)],
        out_specs=[rows_of(tb, d), rows_of(tb, dc), rows_of(tb, d), rows_of(tb, d), whole((8, d))],
        out_shape=[sds((t, d), F32), sds((t, dc), F32), sds((t, d), BF), sds((t, d), BF), sds((8, d), F32)],
        compiler_params=params(60),
        cost_estimate=cost(2 * t * d * (4 * d + 2 * dc), 30 * MIB),
        name="last",
    )(dq, dk, dv, dg, x, c, sp, gm, dcp, g1, g1, g1, g1, g1, g1, sm)


def outer_kernel(a, b, o):
    o[...] = dot_tn(a[...], b[...]).astype(BF)


def outer(a, b):
    t, k = a.shape
    n = b.shape[1]
    kb, nb = min(k, 384), min(n, 768)
    return pl.pallas_call(
        outer_kernel,
        grid=(k // kb, n // nb),
        in_specs=[
            pl.BlockSpec((t, kb), lambda i, j: (0, i)),
            pl.BlockSpec((t, nb), lambda i, j: (0, j)),
        ],
        out_specs=pl.BlockSpec((kb, nb), lambda i, j: (i, j)),
        out_shape=jax.ShapeDtypeStruct((k, n), BF),
        compiler_params=params(60),
        cost_estimate=cost(2 * t * k * n, 2 * (t * k + t * n + k * n)),
        name="outer",
    )(a, b)


def split_rows(w, z):
    return w.reshape(z, w.shape[0] // z, w.shape[1])


def body(ndp, nfs, *args):
    (single, condition, pair_tensor, counts, complex_of, cotangent, condition_gain, scale_weight, scale_bias,
     shift_weight, query_weight, query_bias, key_weight, value_weight, gate_weight, output_weight, pair_gain,
     pair_weight, branch_gate_weight, branch_gate_bias, transition_gain, transition_scale_weight,
     transition_scale_bias, transition_shift_weight, hidden_gate, hidden_value, hidden_output, final_gate_weight,
     final_gate_bias) = args
    copies, rows, d = single.shape
    dc = condition.shape[2]
    t = copies * rows
    heads = pair_weight.shape[1]
    ncomp = counts.shape[0]
    dz = d // nfs
    x = single.reshape(t, d)
    c = condition.reshape(t, dc)
    ct = cotangent.reshape(t, d)
    me = lax.axis_index(DP)
    unit = 16 * ndp

    def padded(total):
        return -(-total // unit) * unit

    def row(v):
        return jnp.pad(v, (0, d - v.shape[0]))[None, :]

    vectors = (scale_bias, query_bias, branch_gate_bias, transition_scale_bias, final_gate_bias,
               condition_gain, transition_gain)
    small = jnp.concatenate([row(v) for v in vectors] + [jnp.zeros((1, d), BF)], axis=0)
    rows1 = 4 * dz + 2 * scale_weight.shape[0]
    pack1 = jnp.concatenate(
        [query_weight, key_weight, value_weight, gate_weight, scale_weight, shift_weight, small], axis=0
    )
    size1 = padded(rows1 + 8)
    pack1 = jnp.pad(pack1, ((0, size1 - pack1.shape[0]), (0, 0)))
    pack2 = jnp.concatenate(
        [hidden_output, output_weight, hidden_gate[:, :d], hidden_gate[:, d:], hidden_value[:, :d],
         hidden_value[:, d:], branch_gate_weight, transition_scale_weight, transition_shift_weight,
         final_gate_weight], axis=0
    )
    rows2 = pack2.shape[0]
    size2 = padded(rows2)
    pack2 = jnp.pad(pack2, ((0, size2 - rows2), (0, 0)))

    def gather(pack):
        n = pack.shape[0] // ndp
        mine = lax.dynamic_slice_in_dim(pack, me * n, n, axis=0)
        return lax.all_gather(mine, (FS, DP), axis=0, tiled=True).reshape(nfs, pack.shape[0], d)

    g1 = gather(pack1)
    g2 = gather(pack2)
    pgain = lax.all_gather(pair_gain, FS, axis=0, tiled=True).astype(F32)
    pw = lax.all_gather(pair_weight, FS, axis=0, tiled=True)
    sm = jnp.transpose(g1[:, rows1 : rows1 + 8, :dz], (1, 0, 2)).reshape(8, d).astype(F32)
    cz = dc // nfs
    gains = jnp.transpose(g1[:, rows1 + 5 : rows1 + 7, :cz], (1, 0, 2)).reshape(2, dc).astype(F32)
    sm = jnp.concatenate([sm[:5], jnp.pad(gains, ((0, 0), (0, d - dc))), sm[7:]], axis=0)

    pair_float = pair_tensor.astype(F32)
    pair_norm, pair_rstd = norm(pair_float)
    pair_low = (pair_norm * pgain).astype(BF)
    bias_local = jnp.transpose(dot(pair_low, pw).astype(BF), (0, 3, 1, 2))
    bias = lax.all_gather(bias_local, FS, axis=3, tiled=True)
    bias = lax.all_gather(bias, DP, axis=2, tiled=True)

    first_in, q, k, v, gp, sp, cl1 = run_first(x, c, g1, sm, rows)
    p, att, gated = run_attend(complex_of, counts, q, k, v, gp, bias, 2)
    (out, gm, dcp, si, act, cl2, gt2, gz2, gh, gv, gsc2, gsh2, gt1, gz1, da, dg, vec_a) = run_middle(
        complex_of, counts, x, c, ct, gated, att, gp, g2, sm, rows // 2
    )
    dq, dk, dv, db = run_attend_back(complex_of, p, q, k, v, da, att, ncomp, 2)
    sgrad, cgrad, gsc1, gsh1, vec_b = run_last(dq, dk, dv, dg, x, c, sp, gm, dcp, g1, sm, rows)

    w_hg = outer(si, gh)
    w_hv = outer(si, gv)
    grads2 = [outer(act, gt2), outer(gated, gt1), w_hg[:, :d], w_hg[:, d:], w_hv[:, :d], w_hv[:, d:],
              outer(c, gz1), outer(cl2, gsc2), outer(cl2, gsh2), outer(c, gz2)]
    pg2 = jnp.concatenate([split_rows(w, nfs) for w in grads2], axis=1)
    pg2 = jnp.pad(pg2, ((0, 0), (0, size2 - rows2), (0, 0)))

    def reduce(pack):
        n = pack.shape[1] // ndp
        part_sum = lax.psum_scatter(
            pack.reshape(nfs * pack.shape[1], d), (FS, DP), scatter_dimension=0, tiled=True
        )
        return lax.all_gather(part_sum, DP, axis=0, tiled=True).astype(F32)

    r2 = reduce(pg2)

    partial_rows = lax.psum_scatter(db, DP, scatter_dimension=2, tiled=True)
    bias_grad = lax.psum_scatter(partial_rows, FS, scatter_dimension=3, tiled=True)
    bias_grad = jnp.transpose(bias_grad, (0, 2, 3, 1))
    pair_width = pair_low.shape[3]
    pw_grad = dot_tn(pair_low.reshape(-1, pair_width), bias_grad.reshape(-1, heads))
    grad_low = dot(bias_grad, pw.T)
    pgain_grad = jnp.sum(grad_low * pair_norm, axis=(0, 1, 2))
    pair_grad = norm_back(pair_norm, pair_rstd, grad_low * pgain)

    vec = (vec_a + vec_b).astype(BF)
    vz = jnp.transpose(vec.reshape(8, nfs, dz), (1, 0, 2))
    cv = jnp.transpose(vec[5:7, :dc].reshape(2, nfs, cz), (1, 0, 2))
    vz = jnp.concatenate(
        [vz[:, :5], jnp.pad(cv, ((0, 0), (0, 0), (0, dz - cz))), jnp.zeros((nfs, 1, dz), BF)], axis=1
    )
    small_grad = jnp.pad(vz, ((0, 0), (0, 0), (0, d - dz)))
    pgz = jnp.pad(pgain_grad.astype(BF).reshape(nfs, 1, -1), ((0, 0), (0, 0), (0, d - pair_width // nfs)))
    pwz = jnp.pad(pw_grad.astype(BF).reshape(nfs, 1, -1), ((0, 0), (0, 0), (0, d - pair_width * heads // nfs)))
    grads1 = [outer(first_in, dq), outer(first_in, dk), outer(first_in, dv), outer(first_in, dg),
              outer(cl1, gsc1), outer(cl1, gsh1)]
    pg1 = jnp.concatenate([split_rows(w, nfs) for w in grads1] + [small_grad, pgz, pwz], axis=1)
    pg1 = jnp.pad(pg1, ((0, 0), (0, size1 - pg1.shape[1]), (0, 0)))
    r1 = reduce(pg1)

    def take(r, at, n):
        return r[at : at + n]

    fz = hidden_output.shape[0]
    o1 = [take(r1, i * dz, dz) for i in range(4)]
    s1 = [take(r1, 4 * dz + i * cz, cz) for i in range(2)]
    sv = r1[rows1 : rows1 + 8]
    ext = r1[rows1 + 8 : rows1 + 10]
    at = fz + 5 * dz
    o2 = [take(r2, fz + i * dz, dz) for i in range(5)]
    c2 = [take(r2, at + i * cz, cz) for i in range(4)]
    shape3 = (copies, rows, d)
    return (
        out.reshape(shape3),
        sgrad.reshape(shape3),
        cgrad.reshape(copies, rows, dc),
        pair_grad,
        sv[5, :cz],
        s1[0],
        sv[0, :dz],
        s1[1],
        o1[0],
        sv[1, :dz],
        o1[1],
        o1[2],
        o1[3],
        o2[0],
        ext[0, : pair_width // nfs],
        ext[1, : pair_width * heads // nfs].reshape(pair_width // nfs, heads),
        c2[0],
        sv[2, :dz],
        sv[6, :cz],
        c2[1],
        sv[3, :dz],
        c2[2],
        jnp.concatenate([o2[1], o2[2]], axis=1),
        jnp.concatenate([o2[3], o2[4]], axis=1),
        take(r2, 0, fz),
        c2[3],
        sv[4, :dz],
    )


def solution(mesh):
    both = (DP, FS)
    wide = P(both, None, None)
    mat = P(FS, None)
    vec = P(FS)
    pair = P(None, DP, FS, None)
    weights = (vec, mat, vec, mat, mat, vec, mat, mat, mat, mat, vec, mat, mat, vec, vec, mat, vec, mat, mat, mat,
               mat, mat, vec)
    in_specs = (wide, wide, pair, P(), P(both), wide) + weights
    out_specs = (wide, wide, wide, pair) + weights
    run = functools.partial(body, mesh.shape[DP], mesh.shape[FS])
    return jax.shard_map(run, mesh=mesh, in_specs=in_specs, out_specs=out_specs, check_vma=False)
```

profile of v0, /device:TPU:1, one launch (start us, length us, event | category | flops | bytes accessed | tf_op | source)
XLA Modules:
  0.0 878.5 jit_solution(8021207284406774566)
XLA Ops:
  7.3 2.7 convert_reduce_fusion
  10.1 3.1 fusion.11
  14.8 10.7 %all-reduce.16 = bf16[128]{0:T(256)(128)(2,1)S(1)} all-reduce(bf16[128]{0:T(256)(128)(2,1)S(1)} %dynamic-update-slice), channel_id=1, replica_groups=mesh['dp'=8,'fsdp'=4] {'fsdp'}, use_global_device_ids=true, to_apply=%add.16 | all-reduce | flops 128 | bytes 512
  25.5 10.2 %all-gather = bf16[4,32,16]{1,2,0:T(8,128)(2,1)S(1)} all-gather(bf16[1,32,16]{1,2,0:T(8,128)(2,1)S(1)} %bitcast.134), channel_id=1, replica_groups=mesh['dp'=8,'fsdp'=4] {'fsdp'}, dimensions={0}, use_global_device_ids=true | all-gather | bytes 5120 | tf_op jit(solution)/shard_map/all_gather | solution.py:503
  36.0 4.0 fusion.19
  40.0 2.1 copy.80
  42.4 11.5 %concatenate.24 = bf16[968,768]{1,0:T(8,128)(2,1)} concatenate(bf16[192,768]{1,0:T(8,128)(2,1)S(1)} %copy-done.16, bf16[192,768]{1,0:T(8,128)(2,1)S(1)} %copy-done.17, bf16[192,768]{1,0:T(8,128)(2,1)} %param.42, bf16[192,768]{1,0:T(8,128)(2,1)} %param.43, bf16[96,768]{1,0:T(8,128)(2,1)} %param.36, bf16[96,768]{1,0:T(8,128)(2,1)} %param.38, bf16[1,768]{1,0:T(2,128)(2,1)S(1)} %broadcast_in_dim.33, ...), dimensions={0} | concatenate | bytes 2973696 | tf_op jit(solution)/shard_map/concatenate | solution.py:481
  55.6 53.3 %all-gather.10.cloned.1.call-done = bf16[2,16,48,384]{2,1,0,3:T(8,128)(2,1)} async-done(((bf16[2,16,48,96]{2,1,0,3:T(8,128)(2,1)}), bf16[2,16,48,384]{2,1,0,3:T(8,128)(2,1)}) %all-gather.10.cloned.1.call-update) | async-done | bytes 1179664 | tf_op jit(solution)/shard_map/all_gather | solution.py:513
  108.9 5.3 copy.81
  116.7 64.2 %all-gather.8.cloned.1.call-done = bf16[4096,768]{1,0:T(8,128)(2,1)} async-done(((bf16[128,768]{1,0:T(8,128)(2,1)}), bf16[4096,768]{1,0:T(8,128)(2,1)}) %all-gather.8.cloned.1.call-update) | async-done | bytes 6291472 | tf_op jit(solution)/shard_map/all_gather | solution.py:498
  183.3 13.0 %first.1 = (bf16[1152,768]{1,0:T(8,128)(2,1)}, bf16[1152,768]{1,0:T(8,128)(2,1)}, bf16[1152,768]{1,0:T(8,128)(2,1)}, bf16[1152,768]{1,0:T(8,128)(2,1)}, bf16[115...) custom-call(bf16[1152,768]{1,0:T(8,128)(2,1)} %bitcast.109, bf16[1152,384]{1,0:T(8,128)(2,1)} %bitcast.104, ...), custom_call_target="tpu_custom_call" | custom-call | flops 6794772480 | bytes 20971520 | tf_op jit(solution)/shard_map/first/pallas_call | solution.py:96
  196.3 44.5 %all-gather.12.cloned.1.call-done.b = bf16[2,16,384,384]{3,2,1,0:T(8,128)(2,1)} async-done(((bf16[2,16,48,384]{3,2,1,0:T(8,128)(2,1)}), bf16[2,16,384,384]{3,2,1,0:T(8,128)(2,1)}) %all-gather.12.cloned.1.call-update) | async-done | bytes 9437200 | tf_op jit(solution)/shard_map/all_gather | solution.py:514
  240.8 21.9 %attend.1 = (bf16[3,16,384,384]{3,2,1,0:T(8,128)(2,1)}, bf16[1152,768]{1,0:T(8,128)(2,1)}, bf16[1152,768]{1,0:T(8,128)(2,1)}) custom-call(s32[3]{0:T(128)} %comp.5, s32[2]{0:T(128)} %cnt.3, bf16[1152,768]{1,0:T(8,128)(2,1)} %get-tuple-element.63.q, bf16[1152,768]{1,0:T(8,128)(2,1)} %get-tuple-element.64.k, bf16[1152,768]{1,0:T(8,128)(2,1)} %get-tuple-element.65.v, ...), custom_call_target="tpu_custom_call" | custom-call | flops 7247757312 | bytes 41943040 | tf_op jit(solution)/shard_map/attend/pallas_call | solution.py:162
  262.6 70.4 %all-gather.14.cloned.1.call-done = bf16[7168,768]{1,0:T(8,128)(2,1)} async-done(((bf16[224,768]{1,0:T(8,128)(2,1)}), bf16[7168,768]{1,0:T(8,128)(2,1)}) %all-gather.14.cloned.1.call-update) | async-done | bytes 11010064 | tf_op jit(solution)/shard_map/all_gather | solution.py:498
  333.0 48.0 %middle.1 = (bf16[1152,768]{1,0:T(8,128)(2,1)}, f32[1152,768]{1,0:T(8,128)}, f32[1152,384]{1,0:T(8,128)}, bf16[1152,768]{1,0:T(8,128)(2,1)}, bf16[1152,1536]{1,0...) custom-call(s32[3]{0:T(128)} %comp.5, s32[2]{0:T(128)} %cnt.3, ...), custom_call_target="tpu_custom_call" | custom-call | flops 24461180928 | bytes 62914560 | tf_op jit(solution)/shard_map/middle/pallas_call | solution.py:356
  381.0 31.9 %attend_back.1 = (bf16[1152,768]{1,0:T(8,128)(2,1)}, bf16[1152,768]{1,0:T(8,128)(2,1)}, bf16[1152,768]{1,0:T(8,128)(2,1)}, bf16[2,16,384,384]{3,2,1,0:T(8,128)(2,1)}) custom-call(s32[3]{0:T(128)} %comp.5, bf16[3,16,384,384]{3,2,1,0:T(8,128)(2,1)} %get-tuple-element.70.p, bf16[1152,768]{1,0:T(8,128)(2,1)} %get-tuple-element.63.q, ...), custom_call_target="tpu_custom_call" | custom-call | flops 14495514624 | bytes 41943040 | tf_op jit(solution)/shard_map/attend_back/pallas_call | solution.py:233
  413.1 3.5 outer.24
  416.6 3.8 outer.25
  420.4 4.1 outer.26
  424.5 5.0 outer.21
  429.5 7.0 outer.20
  436.5 3.9 constant_dynamic-update-slice_fusion.15
  440.4 47.3 %reduce-scatter.7.cloned.1.call-done = bf16[2,16,48,384]{3,2,1,0:T(8,128)(2,1)} async-done(((bf16[2,16,384,384]{3,2,1,0:T(8,128)(2,1)}), bf16[2,16,48,384]{3,2,1,0:T(8,128)(2,1)}) %reduce-scatter.7.cloned.1.call-update) | async-done | bytes 1179664 | tf_op jit(solution)/shard_map/reduce_scatter | solution.py:540
  487.7 5.9 copy.92
  493.6 7.3 reshape.222
  500.9 3.6 outer.27
  505.7 7.5 outer.22
  517.1 7.6 outer.23
  524.7 1.8 fusion.37
  532.3 9.7 %pad.78 = bf16[4,1792,768]{2,1,0:T(8,128)(2,1)} pad(bf16[4,1728,768]{2,1,0:T(8,128)(2,1)} %constant_dynamic-update-slice_fusion.6, bf16[]{:T(256)} %constant.11.clone.1), padding=0_0x0_64x0_0 | pad | bytes 21626882 | tf_op jit(solution)/shard_map/jit(_pad)/pad | solution.py:529
  542.1 18.9 %last.1 = (f32[1152,768]{1,0:T(8,128)}, f32[1152,384]{1,0:T(8,128)}, bf16[1152,768]{1,0:T(8,128)(2,1)}, bf16[1152,768]{1,0:T(8,128)(2,1)}, f32[8,768]{1,0:T(8,128)}) custom-call(bf16[1152,768]{1,0:T(8,128)(2,1)} %get-tuple-element.72.dq.b, bf16[1152,768]{1,0:T(8,128)(2,1)} %get-tuple-element.73.dk.b, bf16[1152,768]{1,0:T(8,128)(2,1)} %get-tuple-element.74.dv.b, ...), custom_call_target="tpu_custom_call" | custom-call | flops 6794772480 | bytes 31457280 | tf_op jit(solution)/shard_map/last/pallas_call | solution.py:411
  562.7 3.7 outer.18
  566.4 3.7 outer.19
  570.1 4.7 outer.14
  574.8 4.7 outer.15
  579.5 4.8 outer.16
  584.2 4.6 outer.17
  592.3 9.8 %fusion.10 = (bf16[128]{0:T(256)(128)(2,1)S(1)}, f32[2,48,96]{2,1,0:T(8,128)}, f32[2,48,96]{2,1,0:T(8,128)}, f32[2,48,96,128]{3,2,1,0:T(8,128)}) fusion(bf16[2,48,96,128]{3,2,1,0:T(8,128)(2,1)S(1)} %copy-done, f32[2,48,96]{2,1,0:T(8,128)S(1)} %copy-done.19, f32[2,48,96]{2,1,0:T(8,128)S(1)} %copy-done.14, f32[128]{0:T(128)S(1)} %convert_element_type.87, ...), kind=kOutput, calls=%fused_computation.12 | convolution fusion | flops 48347008 | bytes 7525120 | tf_op jit(solution)/shard_map/dot_general | solution.py:34
  602.2 5.1 fusion.25
  610.9 35.6 %concatenate.28 = bf16[4,970,768]{2,1,0:T(8,128)(2,1)} concatenate(bf16[4,192,768]{2,1,0:T(8,128)(2,1)} %bitcast.126, bf16[4,192,768]{2,1,0:T(8,128)(2,1)} %bitcast.127, bf16[4,192,768]{2,1,0:T(8,128)(2,1)} %bitcast.128, bf16[4,192,768]{2,1,0:T(8,128)(2,1)} %bitcast.129, bf16[4,96,768]{2,1,0:T(8,128)(2,1)S(1)} %bitcast.118, bf16[4,96,768]{2,1,0:T(8,128)(2,1)S(1)} %bitcast.119, ...), dimensions={1} | concatenate | bytes 11919360 | tf_op jit(solution)/shard_map/concatenate | solution.py:560
  646.4 5.8 pad.77
  652.3 31.6 %reduce-scatter.11.cloned.1.call-done = bf16[224,768]{1,0:T(8,128)(2,1)} async-done(((bf16[7168,768]{1,0:T(8,128)(2,1)}), bf16[224,768]{1,0:T(8,128)(2,1)}) %reduce-scatter.11.cloned.1.call-update) | async-done | bytes 344080 | tf_op jit(solution)/shard_map/reduce_scatter | solution.py:533
  684.0 119.3 %reduce-scatter.9.cloned.1.call-done = bf16[128,768]{1,0:T(8,128)(2,1)} async-done(((bf16[4096,768]{1,0:T(8,128)(2,1)}), bf16[128,768]{1,0:T(8,128)(2,1)}) %reduce-scatter.9.cloned.1.call-update) | async-done | bytes 196624 | tf_op jit(solution)/shard_map/reduce_scatter | solution.py:533
  803.4 11.1 %fusion.9 = f32[2,48,96,128]{3,2,1,0:T(8,128)} fusion(bf16[2,48,96,128]{3,2,1,0:T(8,128)(2,1)S(1)} %copy-done, f32[2,48,96,128]{3,2,1,0:T(8,128)} %get-tuple-element.182, f32[2,48,96]{2,1,0:T(8,128)S(1)} %get-tuple-element.183, f32[2,48,96]{2,1,0:T(8,128)S(1)} %get-tuple-element.184, f32[128]{0:T(128)S(1)} %copy-done.30, f32[2,48,96]{2,1,0:T(8,128)S(1)} %copy-done.20, ...), kind=kLoop, calls=%fused_computation.11 | loop fusion | flops 9437184 | bytes 11944448 | tf_op jit(solution)/shard_map/mul | solution.py:26
  814.6 22.8 %all-gather.18.cloned.1.call-done = bf16[1792,768]{1,0:T(8,128)(2,1)} async-done(((bf16[224,768]{1,0:T(8,128)(2,1)}), bf16[1792,768]{1,0:T(8,128)(2,1)}) %all-gather.18.cloned.1.call-update) | async-done | bytes 2752528 | tf_op jit(solution)/shard_map/all_gather | solution.py:536
  837.4 2.3 slice.207
  839.7 2.1 fusion.35
  844.7 20.4 %all-gather.16.cloned.1.call-done = bf16[1024,768]{1,0:T(8,128)(2,1)} async-done(((bf16[128,768]{1,0:T(8,128)(2,1)}), bf16[1024,768]{1,0:T(8,128)(2,1)}) %all-gather.16.cloned.1.call-update) | async-done | bytes 1572880 | tf_op jit(solution)/shard_map/all_gather | solution.py:536
  (184 shorter events, 36.9 us)
Async XLA Ops:
  7.2 6.1 copy-start.39
  7.2 2.8 copy-start
  7.2 7.3 copy-start.38
  7.2 18.3 %copy-start.28 = (bf16[32,16]{0,1:T(8,128)(2,1)S(1)}, bf16[32,16]{0,1:T(8,128)(2,1)}, u32[]{:S(2)}) copy-start(bf16[32,16]{0,1:T(8,128)(2,1)} %param.46) | copy-start | bytes 3076
  7.2 101.6 %all-gather.10.cloned.1.call-start = ((), (), s32[]{:S(2)}) async-start(), calls=%async_computation.5 | async-start | bytes 3932160 | tf_op jit(solution)/shard_map/all_gather | solution.py:513
  10.1 29.9 %copy-start.13 = (f32[2,48,96]{2,1,0:T(8,128)}, f32[2,48,96]{2,1,0:T(8,128)S(1)}, u32[]{:S(2)}) copy-start(f32[2,48,96]{2,1,0:T(8,128)S(1)} %broadcast_multiply_fusion.2) | copy-start | bytes 110596
  13.2 26.7 %copy-start.18 = (f32[2,48,96]{2,1,0:T(8,128)}, f32[2,48,96]{2,1,0:T(8,128)S(1)}, u32[]{:S(2)}) copy-start(f32[2,48,96]{2,1,0:T(8,128)S(1)} %add_rsqrt_fusion) | copy-start | bytes 110596
  25.5 566.8 %copy-start.29 = (f32[128]{0:T(128)}, f32[128]{0:T(128)S(1)}, u32[]{:S(2)}) copy-start(f32[128]{0:T(128)S(1)} %convert_element_type.87) | copy-start | bytes 1540
  35.9 6.3 copy-start.31
  35.9 6.3 copy-start.32
  35.9 6.3 copy-start.33
  35.9 6.4 copy-start.34
  35.9 6.4 copy-start.35
  35.9 6.4 copy-start.36
  35.9 6.4 copy-start.37
  35.9 6.5 copy-start.16
  36.0 6.5 copy-start.17
  42.1 138.9 %all-gather.8.cloned.1.call-start = ((), (), s32[]{:S(2)}) async-start(), calls=%async_computation.4 | async-start | bytes 6488064 | tf_op jit(solution)/shard_map/all_gather | solution.py:498
  55.5 58.7 %copy-start.10 = (bf16[384,768]{1,0:T(8,128)(2,1)S(1)}, bf16[384,768]{1,0:T(8,128)(2,1)}, u32[]{:S(2)}) copy-start(bf16[384,768]{1,0:T(8,128)(2,1)} %param.55) | copy-start | bytes 1769476
  55.6 59.9 %copy-start.11 = (bf16[192,1536]{1,0:T(8,128)(2,1)S(1)}, bf16[192,1536]{1,0:T(8,128)(2,1)}, u32[]{:S(2)}) copy-start(bf16[192,1536]{1,0:T(8,128)(2,1)} %param.53) | copy-start | bytes 1769476
  55.6 185.2 %all-gather.12.cloned.1.call-start = ((), (), s32[]{:S(2)}) async-start(), calls=%async_computation.6 | async-start | bytes 10616832 | tf_op jit(solution)/shard_map/all_gather | solution.py:514
  114.2 218.8 %all-gather.14.cloned.1.call-start = ((), (), s32[]{:S(2)}) async-start(), calls=%async_computation.7 | async-start | bytes 11354112 | tf_op jit(solution)/shard_map/all_gather | solution.py:498
  114.3 1.3 copy-start.22
  114.3 1.3 copy-start.23
  114.3 1.4 copy-start.24
  116.5 371.2 %reduce-scatter.7.cloned.1.call-start = ((), (), s32[]{:S(2)}) async-start(), calls=%async_computation.8 | async-start | bytes 10616832 | tf_op jit(solution)/shard_map/reduce_scatter | solution.py:540
  413.0 175.8 %reduce-scatter.13.cloned.1.call-start = ((), (), s32[]{:S(2)}) async-start(), calls=%async_computation.13 | async-start | bytes 1474560
  500.9 3.7 copy-start.9
  500.9 183.0 %reduce-scatter.11.cloned.1.call-start = ((), (), s32[]{:S(2)}) async-start(), calls=%async_computation.11 | async-start | bytes 11354112 | tf_op jit(solution)/shard_map/reduce_scatter | solution.py:533
  526.5 2.3 copy-start.7
  526.5 3.1 copy-start.6
  527.6 2.9 copy-start.5
  527.6 3.8 copy-start.8
  542.0 261.3 %reduce-scatter.9.cloned.1.call-start = ((), (), s32[]{:S(2)}) async-start(), calls=%async_computation.9 | async-start | bytes 6488064 | tf_op jit(solution)/shard_map/reduce_scatter | solution.py:533
  542.1 18.9 %copy-start.27 = (f32[8,768]{1,0:T(8,128)S(1)}, f32[8,768]{1,0:T(8,128)}, u32[]{:S(2)}) copy-start(f32[8,768]{1,0:T(8,128)} %get-tuple-element.86) | copy-start | bytes 73732
  584.2 8.1 copy-start.14
  584.2 8.1 copy-start.19
  602.2 8.7 copy-start.3
  602.2 8.6 copy-start.4
  652.2 151.2 %copy-start.25 = (f32[2,48,96]{2,1,0:T(8,128)S(1)}, f32[2,48,96]{2,1,0:T(8,128)}, u32[]{:S(2)}) copy-start(f32[2,48,96]{2,1,0:T(8,128)} %get-tuple-element.154) | copy-start | bytes 110596
  652.2 151.2 %copy-start.26 = (f32[2,48,96]{2,1,0:T(8,128)S(1)}, f32[2,48,96]{2,1,0:T(8,128)}, u32[]{:S(2)}) copy-start(f32[2,48,96]{2,1,0:T(8,128)} %get-tuple-element.155) | copy-start | bytes 110596
  652.2 151.2 %copy-start.15 = (f32[2,48,96]{2,1,0:T(8,128)S(1)}, f32[2,48,96]{2,1,0:T(8,128)}, u32[]{:S(2)}) copy-start(f32[2,48,96]{2,1,0:T(8,128)} %copy-done.13) | copy-start | bytes 110596
  652.2 151.2 %copy-start.20 = (f32[2,48,96]{2,1,0:T(8,128)S(1)}, f32[2,48,96]{2,1,0:T(8,128)}, u32[]{:S(2)}) copy-start(f32[2,48,96]{2,1,0:T(8,128)} %copy-done.18) | copy-start | bytes 110596
  652.2 151.2 %copy-start.30 = (f32[128]{0:T(128)S(1)}, f32[128]{0:T(128)}, u32[]{:S(2)}) copy-start(f32[128]{0:T(128)} %copy-done.29) | copy-start | bytes 1540
  652.3 185.1 %all-gather.18.cloned.1.call-start = ((), (), s32[]{:S(2)}) async-start(), calls=%async_computation.12 | async-start | bytes 3096576 | tf_op jit(solution)/shard_map/all_gather | solution.py:536
  684.0 181.1 %all-gather.16.cloned.1.call-start = ((), (), s32[]{:S(2)}) async-start(), calls=%async_computation.10 | async-start | bytes 1769472 | tf_op jit(solution)/shard_map/all_gather | solution.py:536
  837.4 4.5 copy-start.2
  865.0 3.6 copy-start.1
  (2 other events, 2.5 us)
Sparse Core Ops, SparseCore 0:
  42.2 66.6 all-gather.9
  112.3 68.6 all-gather.7
  183.5 57.2 all-gather.11
  244.1 88.9 all-gather.13
  413.1 74.4 reduce-scatter.6
  501.0 28.9 reduce-scatter.12
  542.1 141.7 reduce-scatter.10
  689.6 113.7 reduce-scatter.8
  805.4 31.9 all-gather.17
  839.3 25.6 all-gather.15
where the time goes:
time: 886 us; the launch traced here: 878 us
  waiting for transfers between devices  474 us (53%)
  Pallas kernels  202 us (23%)
  local copies, waits for them, and re-layouts  124 us (14%)
  other arithmetic  22.7 us (3%)
  blocking collectives  21 us (2%)
  matrix products  18.9 us (2%)
  between operations  15.8 us (2%)
    reduce_scatter x2, waiting for transfers between devices, reduce(): lax.psum_scatter(pack.reshape(nfs * pack.shape[1], d), (FS, DP), scatter_...  151 us
    all_gather x2, waiting for transfers between devices, gather(): lax.all_gather(mine, (FS, DP), axis=0, tiled=True)  135 us
    pallas_call x14, Pallas kernels, outer(): pl.pallas_call(outer_kernel, grid=(k // kb, n // nb), in_specs=[pl.BlockS...  68.2 us
    all_gather x1, waiting for transfers between devices, body(): bias = lax.all_gather(bias_local, FS, axis=3, tiled=True)  53.3 us
    pallas_call x1, Pallas kernels, run_middle(): pl.pallas_call(functools.partial(middle_kernel, per_copy), grid_spec=pltp...  48 us
    reduce_scatter x1, waiting for transfers between devices, body(): partial_rows = lax.psum_scatter(db, DP, scatter_dimension=2, tiled=True)  47.3 us
    all_gather x1, waiting for transfers between devices, body(): bias = lax.all_gather(bias, DP, axis=2, tiled=True)  44.5 us
    all_gather x2, waiting for transfers between devices, reduce(): return lax.all_gather(part_sum, DP, axis=0, tiled=True).astype(F32)  43.2 us
  transfers between devices with their start and end apart: 10, of which 9 were waited for; matrix products, arithmetic and copies ran while one was open for 15% of the time, Pallas kernels for 14%

commit v1 on v0

--- a/solution.py
+++ b/solution.py
@@ -128,10 +128,8 @@
         acc[key] = piece if key not in acc else acc[key] + piece
 
 
-def attend_kernel(per, hs, comp, cnt, q, k, v, b, gp, p_out, att, gated):
-    n = comp[pl.program_id(0)]
+def attend_body(per, hs, limit, q, k, v, bias_of, gp, keep, att, gated):
     width = min(256, per * hs)
-    limit = cnt[n]
     mrow = jnp.where(
         lax.broadcasted_iota(jnp.int32, (1, k.shape[0]), 1) < limit, 0.0, NEGATIVE
     ).astype(F32)
@@ -140,15 +138,23 @@
     for j, (w, o) in enumerate(windows(per, hs)):
         m = lane_mask(o, hs, width)
         s = dot_nt(q[:, w : w + width] * m, k[:, w : w + width]) * scale
-        s = s + (b[0, j].astype(F32) + mrow)
+        s = s + (bias_of(j).astype(F32) + mrow)
         e = jnp.exp(s - jnp.max(s, axis=-1, keepdims=True))
         pb = (e * (1.0 / jnp.sum(e, axis=-1, keepdims=True))).astype(BF)
-        p_out[0, j] = pb
+        keep(j, pb)
         put(acc, w, width, dot(pb, v[:, w : w + width] * m))
     for key, val in acc.items():
         cols = slice(128 * key, 128 * key + 128)
         att[:, cols] = val.astype(BF)
         gated[:, cols] = (sig(gp[:, cols].astype(F32)) * val).astype(BF)
+
+
+def attend_kernel(per, hs, comp, cnt, q, k, v, b, gp, p_out, att, gated):
+    def keep(j, val):
+        p_out[0, j] = val
+
+    limit = cnt[comp[pl.program_id(0)]]
+    attend_body(per, hs, limit, q, k, v, lambda j: b[0, j], gp, keep, att, gated)
 
 
 def run_attend(comp, cnt, q, k, v, gp, bias, groups):
@@ -373,7 +379,7 @@
     )(comp, cnt, x, c, ct, gat, att, gp, g2, g2, g2, g2, g2, g2, g2, g2, g2, g2, sm)
 
 
-def last_kernel(dq, dk, dv, dg, x, c, sp, gm, dcp, wq, wk, wv, wg, ws, wh, sm, sg_o, cg_o, gsc_o, gsh_o, vec):
+def last_body(dq, dk, dv, dg, x, c, sp, gm, dcp, wq, wk, wv, wg, ws, wh, sm, sg_o, cg_o, gsc_o, gsh_o, vec):
     dc = c.shape[1]
     e = (
         dot_nt(dq[...], flat(wq))
@@ -392,14 +398,17 @@
     gc = dot_nt(gsc, flat(ws)) + dot_nt(gsh, flat(wh))
     cn, cr = norm(c[...].astype(F32))
     cg_o[...] = dcp[...] + norm_back(cn, cr, gc * sm[5:6, :dc])
-
-    @pl.when(pl.program_id(0) == 0)
-    def _():
-        vec[...] = jnp.zeros_like(vec)
-
     vec[0:1, :] += colsum(gsc)
     vec[1:2, :] += colsum(dq[...])
     vec[5:6, :dc] += jnp.sum(gc * cn, axis=0, keepdims=True)
+
+
+def last_kernel(*refs):
+    @pl.when(pl.program_id(0) == 0)
+    def _():
+        refs[-1][...] = jnp.zeros_like(refs[-1])
+
+    last_body(*refs)
 
 
 def run_last(dq, dk, dv, dg, x, c, sp, gm, dcp, g1, sm, tb):
@@ -423,31 +432,1059 @@
     )(dq, dk, dv, dg, x, c, sp, gm, dcp, g1, g1, g1, g1, g1, g1, sm)
 
 
-def outer_kernel(a, b, o):
-    o[...] = dot_tn(a[...], b[...]).astype(BF)
-
-
-def outer(a, b):
-    t, k = a.shape
-    n = b.shape[1]
-    kb, nb = min(k, 384), min(n, 768)
+def flip(i, b):
+    return i + b * (1 - 2 * ((i // b) % 2))
+
+
+def flips(i, bs):
+    for b in bs:
+        i = flip(i, b)
+    return i
+
+
+def subsets(bs):
+    out = [()]
+    for b in bs:
+        out = out + [s + (b,) for s in out]
+    return out
+
+
+def bits_of(n):
+    out, b = [], 1
+    while b < n:
+        out.append(b)
+        b *= 2
+    return out
+
+
+def peers(ndp, nfs):
+    return nfs - 1 + len(bits_of(ndp))
+
+
+class Plan:
+    def __init__(self, ndp, nfs, send, recv, local):
+        self.ndp, self.nfs, self.send, self.recv, self.lsem = ndp, nfs, send, recv, local
+        self.dp, self.z = lax.axis_index(DP), lax.axis_index(FS)
+        self.sent, self.locals = [], 0
+
+    def barrier(self):
+        sem = pltpu.get_barrier_semaphore()
+        to = [(self.dp, (self.z + k) % self.nfs) for k in range(1, self.nfs)]
+        to += [(flip(self.dp, b), self.z) for b in bits_of(self.ndp)]
+        for dev in to:
+            pl.semaphore_signal(sem, inc=1, device_id=dev, device_id_type=pl.DeviceIdType.MESH)
+        pl.semaphore_wait(sem, len(to))
+
+    def copy(self, src, dst, dp, z):
+        n = len(self.sent)
+        c = pltpu.make_async_remote_copy(
+            src_ref=src, dst_ref=dst, send_sem=self.send.at[n], recv_sem=self.recv.at[n], device_id=(dp, z),
+            device_id_type=pl.DeviceIdType.MESH,
+        )
+        self.sent.append(c)
+        return c
+
+    def here(self, src, dst):
+        self.locals += 1
+        return pltpu.make_async_copy(src, dst, self.lsem.at[self.locals - 1])
+
+    def finish(self):
+        for c in self.sent:
+            c.wait_send()
+
+
+def start(cs):
+    for c in cs:
+        c.start()
+
+
+def arrive(cs):
+    for c in cs:
+        c.wait_recv()
+
+
+def spread(plan, halves, slot, own, first, extra):
+    k = len(halves[0][1])
+    chips, sibs = [], []
+    fresh = [(part_, ()) for part_, _ in halves]
+    for s in range(k + 1):
+        sibs.append([])
+        for part_, sub in fresh:
+            e = flips(plan.dp, sub)
+            src = slot(part_, e) if sub else own(part_)
+            sibs[-1].append(plan.copy(src, slot(part_, e), flip(plan.dp, 1), plan.z))
+        if s == k:
+            break
+        chips.append([])
+        for part_, order in halves:
+            for sub in subsets(order[:s]):
+                e = flips(plan.dp, sub)
+                src = slot(part_, e) if sub else own(part_)
+                chips[-1].append(plan.copy(src, slot(part_, e), flip(plan.dp, order[s]), plan.z))
+        fresh = [(p_, sub + (order[s],)) for p_, order in halves for sub in subsets(order[:s])]
+
+    def opening():
+        first()
+        if k:
+            start(chips[0])
+        start(sibs[0])
+
+    def middle(s):
+        def step():
+            arrive(chips[s - 1])
+            if s < k:
+                start(chips[s])
+            start(sibs[s])
+
+        return step
+
+    def closing():
+        for group in sibs:
+            arrive(group)
+        extra()
+
+    return [opening] + [middle(s) for s in range(1, k + 1)] + [closing]
+
+
+def two_orders(ndp):
+    bs = [2 * b for b in bits_of(ndp // 2)]
+    return bs, bs[::-1]
+
+
+def gather_steps(plan, shard, g, ready):
+    nfs, n = plan.nfs, g.shape[1] // plan.ndp
+    mine = shard.at[pl.ds(plan.dp * n, n), :]
+    here = g.at[plan.z, pl.ds(plan.dp * n, n), :]
+    own = plan.here(mine, here)
+    zs = [plan.copy(mine, here, plan.dp, (plan.z + k) % nfs) for k in range(1, nfs)]
+    hz = nfs // 2
+    up, down = two_orders(plan.ndp)
+    halves = [(pl.ds(0, hz), up), (pl.ds(hz, nfs - hz), down)]
+
+    def slot(part_, e):
+        return g.at[part_, pl.ds(e * n, n), :]
+
+    def begin():
+        ready()
+        start(zs)
+        own.start()
+
+    def landed():
+        own.wait()
+        arrive(zs)
+
+    rest = spread(plan, halves, slot, lambda p_: slot(p_, plan.dp), landed, lambda: None)
+    return [begin] + rest
+
+
+def place(cw, full, at, rows_first):
+    a = lax.broadcasted_iota(jnp.int32, (cw, full) if rows_first else (full, cw), 0)
+    b = lax.broadcasted_iota(jnp.int32, (cw, full) if rows_first else (full, cw), 1)
+    hit = b == a + at if rows_first else a == b + at
+    return jnp.where(hit, 1.0, 0.0).astype(BF)
+
+
+def bias_gather_steps(plan, bl, zb, bias):
+    nfs = plan.nfs
+    nh, r, cw = bl.shape
+    full = cw * nfs
+    own = plan.here(bl, zb.at[plan.z])
+    mine = pl.ds(pl.multiple_of(plan.dp * r, r), r)
+    zs = [plan.copy(bl, zb.at[plan.z], plan.dp, (plan.z + k) % nfs) for k in range(1, nfs)]
+    up, down = two_orders(plan.ndp)
+    hh = nh // 2
+    halves = [(pl.ds(0, hh), up), (pl.ds(hh, nh - hh), down)]
+
+    def begin():
+        own.start()
+        start(zs)
+
+    def join():
+        own.wait()
+        arrive(zs)
+
+        def some(i, carry):
+            total = None
+            for zz in range(nfs):
+                v = zb[zz, pl.ds(i * 8, 8)].reshape(8 * r, cw)
+                term = dot(v, place(cw, full, zz * cw, True))
+                total = term if total is None else total + term
+            bias[pl.ds(i * 8, 8), mine, :] = total.astype(BF).reshape(8, r, full)
+            return carry
+
+        lax.fori_loop(0, nh // 8, some, 0)
+
+    def slot(p_, e):
+        return bias.at[p_, pl.ds(e * r, r), :]
+
+    rest = spread(plan, halves, slot, lambda p_: slot(p_, plan.dp), join, lambda: None)
+    return [begin] + rest
+
+
+def add_rows(dst, src):
+    def one(i, carry):
+        dst[i] = dst[i] + src[i]
+        return carry
+
+    lax.fori_loop(0, dst.shape[0], one, 0)
+
+
+def sum_steps(plan, piece, acc, crecv, rbuf, cut, ready):
+    nchip = acc.shape[0]
+    dp, z = plan.dp, plan.z
+    m, core = dp // 2, dp % 2
+    cs = [plan.copy(piece(2 * f + 1 - core), crecv.at[f], flip(dp, 1), z) for f in range(nchip)]
+    ls = [plan.here(piece(2 * f + core), acc.at[f]) for f in range(nchip)]
+    bs = bits_of(nchip)
+    orders = (bs, bs[::-1])
+    rounds = []
+    at = [0, 0]
+    for s in range(len(bs)):
+        rounds.append([])
+        for h, order in enumerate(orders):
+            part_ = pl.ds(*cut[h])
+            for sub in subsets(order[s + 1 :]):
+                f = flips(m, (order[s],) + sub)
+                c = plan.copy(acc.at[f, part_], rbuf.at[at[h], part_], flip(dp, 2 * order[s]), z)
+                rounds[-1].append((c, flips(m, sub), at[h], part_))
+                at[h] += 1
+
+    def begin():
+        ready()
+        start(cs)
+        start(ls)
+
+    def pair():
+        for f in range(nchip):
+            ls[f].wait()
+            cs[f].wait_recv()
+            add_rows(acc.at[f], crecv.at[f])
+        if rounds:
+            start([c[0] for c in rounds[0]])
+
+    def chip(s):
+        def step():
+            for c, f, o, part_ in rounds[s - 1]:
+                c.wait_recv()
+                add_rows(acc.at[f, part_], rbuf.at[o, part_])
+            if s < len(bs):
+                start([c[0] for c in rounds[s]])
+
+        return step
+
+    return [begin, pair] + [chip(s) for s in range(1, len(bs) + 1)]
+
+
+def join_steps(one, two):
+    def both():
+        one[-1]()
+        two[0]()
+
+    return one[:-1] + [both] + two[1:]
+
+
+def reduce_steps(plan, pg, out, acc, crecv, rbuf, zr, fin, ready):
+    nfs, n = plan.nfs, acc.shape[2]
+    dp, z = plan.dp, plan.z
+    hz = nfs // 2
+    sums = sum_steps(plan, lambda e: pg.at[:, pl.ds(e * n, n), :], acc, crecv, rbuf, ((0, hz), (hz, nfs - hz)), ready)
+    zs = [plan.copy(acc.at[dp // 2, (z + k) % nfs], zr.at[k - 1], dp, (z + k) % nfs) for k in range(1, nfs)]
+    keep = plan.here(fin, out.at[pl.ds(dp * n, n), :])
+    w = fin.shape[1] // 2
+    up, down = two_orders(plan.ndp)
+    halves = [(pl.ds(0, w), up), (pl.ds(w, w), down)]
+
+    def total():
+        arrive(zs)
+        t = acc[dp // 2, z].astype(F32)
+        for k in range(nfs - 1):
+            t = t + zr[k].astype(F32)
+        fin[...] = t.astype(BF)
+        keep.start()
+
+    rest = spread(plan, halves, lambda p_, e: out.at[pl.ds(e * n, n), p_], lambda p_: fin.at[:, p_], total, keep.wait)
+    return join_steps(sums, [lambda: start(zs)]) + rest
+
+
+def bias_reduce_steps(plan, db, out, acc, crecv, rbuf, zs, zr):
+    nfs = plan.nfs
+    dp, z = plan.dp, plan.z
+    nchip, nh, r, full = acc.shape
+    cw = full // nfs
+    hh = nh // 2
+    sums = sum_steps(plan, lambda e: db.at[:, pl.ds(e * r, r), :], acc, crecv, rbuf, ((0, hh), (hh, nh - hh)), lambda: None)
+    to = [plan.copy(zs.at[(z + k) % nfs], zr.at[k - 1], dp, (z + k) % nfs) for k in range(1, nfs)]
+
+    def cut():
+        def some(i, carry):
+            v = acc[dp // 2, pl.ds(i * 8, 8)].reshape(8 * r, full)
+            for zz in range(nfs):
+                zs[zz, pl.ds(i * 8, 8)] = dot(v, place(cw, full, zz * cw, False)).astype(BF).reshape(8, r, cw)
+            return carry
+
+        lax.fori_loop(0, nh // 8, some, 0)
+        start(to)
+
+    def total():
+        arrive(to)
+
+        def one(i, carry):
+            t = zs[z, i].astype(F32)
+            for k in range(nfs - 1):
+                t = t + zr[k, i].astype(F32)
+            out[i] = t.astype(BF).astype(F32)
+            return carry
+
+        lax.fori_loop(0, nh, one, 0)
+
+    return join_steps(sums, [cut]) + [total]
+
+
+DMA = pltpu.SemaphoreType.DMA
+
+
+def pair_params(tg):
+    m = tg[...].reshape(128, 128)
+    rows = dot_tn(m, place(128, 128, 0, True))
+    return rows[0:16].astype(BF), rows[16:17]
+
+
+def pair_rows(pair, n, i):
+    x = pair[n, pl.ds(i * 16, 16)].astype(F32)
+    return norm(x.reshape(x.shape[0] * x.shape[1], x.shape[2]))
+
+
+def pair_steps(plan, pair, tp, tg, bl):
+    nfs = plan.nfs
+    ncomp, r, cw, _ = pair.shape
+    zs = [plan.copy(tp, tg.at[plan.z], plan.dp, (plan.z + k) % nfs) for k in range(1, nfs)]
+
+    def begin():
+        tg[plan.z] = tp[...]
+        start(zs)
+
+    def work(n):
+        def step():
+            if n == 0:
+                arrive(zs)
+            pw, gain = pair_params(tg)
+            heads = pw.shape[0]
+
+            def some(i, carry):
+                pn, _ = pair_rows(pair, n, i)
+                low = (pn * gain).astype(BF)
+                parts = [dot_nt(pw, low[cw * k : cw * k + cw]) for k in range(16)]
+                v = jnp.transpose(jnp.stack(parts), (1, 0, 2))
+                bl[pl.ds(n * heads, heads), pl.ds(i * 16, 16), :] = v.astype(BF)
+                return carry
+
+            lax.fori_loop(0, r // 16, some, 0)
+
+        return step
+
+    return [begin] + [work(n) for n in range(ncomp)]
+
+
+def pair_back(pair_hbm, tg, ob, pgrad, tacc):
+    ncomp, r, cw, width = pair_hbm.shape
+    pw, gain = pair_params(tg)
+    heads = pw.shape[0]
+    per = r // 16
+
+    def run(pair, pgb, lsem, osem):
+        load = pltpu.make_async_copy(pair_hbm, pair, lsem.at[0])
+        load.start()
+        load.wait()
+
+        def flight(it):
+            return pltpu.make_async_copy(pgb.at[it % 2], pgrad.at[it // per, pl.ds(it % per * 16, 16)], osem.at[it % 2])
+
+        def some(it, carry):
+            pwg, pgg = carry
+            n, i = it // per, it % per
+            pn, pr = pair_rows(pair, n, i)
+            low = (pn * gain).astype(BF)
+            g = jnp.transpose(ob[pl.ds(n * heads, heads), pl.ds(i * 16, 16), :], (1, 0, 2)).astype(BF)
+            parts = []
+            for k in range(16):
+                parts.append(dot_tn(g[k], pw))
+                pwg = pwg + dot(g[k], low[cw * k : cw * k + cw])
+            gl = jnp.concatenate(parts, axis=0)
+            pgg = pgg + jnp.sum(gl * pn, axis=0, keepdims=True)
+
+            @pl.when(it >= 2)
+            def _():
+                flight(it - 2).wait()
+
+            pgb[it % 2] = norm_back(pn, pr, gl * gain).reshape(16, cw, width)
+            flight(it).start()
+            return pwg, pgg
+
+        zero = (jnp.zeros((heads, width), F32), jnp.zeros((1, width), F32))
+        pwg, pgg = lax.fori_loop(0, ncomp * per, some, zero)
+        for it in range(max(ncomp * per - 2, 0), ncomp * per):
+            flight(it).wait()
+        tacc[0, 0:16, :] = pwg
+        tacc[0, 16:32, :] = jnp.broadcast_to(pgg, (16, width))
+
+    pl.run_scoped(run, pltpu.VMEM(pair_hbm.shape, BF), pltpu.VMEM((2, 16, cw, width), F32), DMA((1,)), DMA((2,)))
+
+
+def tiny_steps(plan, tacc, tr, tz, out, work):
+    nfs = plan.nfs
+    bs = bits_of(plan.ndp)
+    cs = [plan.copy(tacc.at[i], tr.at[i], flip(plan.dp, b), plan.z) for i, b in enumerate(bs)]
+    zs = [plan.copy(tacc.at[len(bs)], tz.at[k - 1], plan.dp, (plan.z + k) % nfs) for k in range(1, nfs)]
+
+    def begin():
+        work()
+        cs[0].start()
+
+    def step(i):
+        def go():
+            cs[i].wait_recv()
+            tacc[i + 1] = tacc[i] + tr[i]
+            start([cs[i + 1]] if i + 1 < len(bs) else zs)
+
+        return go
+
+    def total():
+        arrive(zs)
+        t = tacc[len(bs)]
+        for k in range(nfs - 1):
+            t = t + tz[k]
+        out[...] = t
+
+    return [begin] + [step(i) for i in range(len(bs))] + [total]
+
+
+ANYWHERE = pl.BlockSpec(memory_space=pl.ANY)
+def follow(order, lists):
+    at = {k: 0 for k in lists}
+    for ch in order:
+        if ch in lists and at[ch] < len(lists[ch]):
+            lists[ch][at[ch]]()
+            at[ch] += 1
+    for k, steps in lists.items():
+        for step in steps[at[k] :]:
+            step()
+
+
+VMEM = pl.BlockSpec(memory_space=pltpu.VMEM)
+SMEM = pl.BlockSpec(memory_space=pltpu.SMEM)
+
+
+def fill_vectors(small, s1, rows1):
+    parts = [v[...].astype(F32) for v in small]
+    v = jnp.concatenate(parts[:5] + [jnp.concatenate(parts[5:], axis=1)], axis=0)
+    pad = jnp.zeros((16 - v.shape[0], v.shape[1]), F32)
+    s1[rows1 : rows1 + 16, 0 : v.shape[1]] = jnp.concatenate([v, pad], axis=0).astype(BF)
+
+
+def forward_parts(plan, rows1, comp, cnt, x, c, g1, sm, outs, bias, wv, vs, pst, psem, fsem, during, within):
+    nfs = plan.nfs
+    copies = comp.shape[0]
+    t, d = x.shape
+    dc = c.shape[1]
+    rows = t // copies
+    dz, cz = d // nfs, dc // nfs
+    heads = outs[-1].shape[1]
+    groups = 2
+    per, dg, hs = heads // groups, d // groups, d // heads
+    load = plan.here(g1, wv)
+    leave = [pltpu.make_async_copy(v, o, fsem.at[i]) for i, (v, o) in enumerate(zip(vs, outs))]
+    fi, q, k, v, gp, sp, cl, att, gated = vs
+    p = outs[-1]
+
+    def vectors():
+        parts = [jnp.zeros((16, d), F32), jnp.zeros((16, dc), F32), jnp.zeros((16, dc), F32)]
+        a = lax.broadcasted_iota(jnp.int32, (dz, dc), 0)
+        b = lax.broadcasted_iota(jnp.int32, (dz, dc), 1)
+        for z in range(nfs):
+            piece = wv[z, rows1 : rows1 + 16, :][:, :dz]
+            one = jnp.where((a < cz) & (b == a + z * cz), 1.0, 0.0).astype(BF)
+            two = jnp.where((a >= cz) & (b == a - cz + z * cz), 1.0, 0.0).astype(BF)
+            for i, e in enumerate((place(dz, d, z * dz, True), one, two)):
+                parts[i] = parts[i] + dot(piece, e)
+        sm[...] = parts[0][0:8]
+        sm[5:6, 0:dc] = parts[1][5:6]
+        sm[6:7, 0:dc] = parts[2][5:6]
+
+    def first():
+        load.start()
+        load.wait()
+        vectors()
+
+        def one(i, carry):
+            at = pl.ds(pl.multiple_of(i * rows, rows), rows)
+
+            def view(ref):
+                return ref.at[at, :]
+
+            ws = [wv.at[:, pl.ds(j * dz, dz), :] for j in range(4)]
+            ws += [wv.at[:, pl.ds(4 * dz + j * cz, cz), :] for j in range(2)]
+            first_kernel(view(x), view(c), *ws, sm, *[view(o) for o in vs[:7]])
+            for at_i, step in during.items():
+                pl.when(i == at_i)(step)
+            return carry
+
+        lax.fori_loop(0, copies, one, 0)
+        start(leave[:7])
+
+    def flight(it):
+        return pltpu.make_async_copy(pst.at[it % 2], p.at[it // groups, pl.ds(it % groups * per, per)], psem.at[it % 2])
+
+    def attend():
+        def one(it, carry):
+            ci, g = it // groups, it % groups
+            at = pl.ds(pl.multiple_of(ci * rows, rows), rows)
+            cols = pl.ds(pl.multiple_of(g * dg, dg), dg)
+            n = comp[ci]
+
+            @pl.when(it >= 2)
+            def _():
+                flight(it - 2).wait()
+
+            def keep(j, val):
+                pst[it % 2, j] = val
+
+            def view(ref):
+                return ref.at[at, cols]
+
+            attend_body(per, hs, cnt[n], view(q), view(k), view(v), lambda j: bias[n * heads + g * per + j], view(gp),
+                        keep, view(att), view(gated))
+            flight(it).start()
+            pl.when(it == copies * groups // 2)(within)
+            return carry
+
+        lax.fori_loop(0, copies * groups, one, 0)
+        start(leave[7:])
+
+    def leaving():
+        for it in range(copies * groups - 2, copies * groups):
+            flight(it).wait()
+        for o in leave:
+            o.wait()
+
+    return first, attend, leaving
+
+
+def gather_kernel(ndp, nfs, spots, rows1, with_bias, *refs):
+    nw = len(spots)
+    ws, small, rest = refs[:nw], refs[nw : nw + 7], refs[nw + 7 :]
+    if with_bias:
+        pair, tp, comp, cnt, x, c, g1, g2, tg, sm = rest[:10]
+        outs, rest = rest[10:20], rest[20:]
+        s1, s2, bl, zb, bias, wv, pst = rest[:7]
+        vs = rest[7:16]
+        send, recv, local, psem, fsem = rest[16:]
+    else:
+        g1, g2, s1, s2, send, recv, local = rest
+    plan = Plan(ndp, nfs, send, recv, local)
+    fill = {0: [], 1: []}
+    for w, (which, col, width, at) in zip(ws, spots):
+        src = w if width == w.shape[1] else w.at[:, pl.ds(col, width)]
+        fill[which].append(plan.here(src, (s1, s2)[which].at[pl.ds(at, w.shape[0]), :]))
+    start(fill[0])
+    start(fill[1])
+    fill_vectors(small, s1, rows1)
+    plan.barrier()
+
+    def wait(cs):
+        def go():
+            for c in cs:
+                c.wait()
+
+        return go
+
+    size1 = g1.shape[1]
+    half = size1 // 2
+    nothing = wait([])
+    if half % (16 * ndp) == 0:
+        spans = [pl.ds(0, half), pl.ds(half, half)]
+    else:
+        spans = [pl.ds(0, size1)]
+    a = [gather_steps(plan, s1.at[sp_], g1.at[:, sp_], nothing if i else wait(fill[0])) for i, sp_ in enumerate(spans)]
+    c_ = gather_steps(plan, s2, g2, wait(fill[1]))
+    if not with_bias:
+        follow("", dict(enumerate(a + [c_])))
+        plan.finish()
+        return
+    p = pair_steps(plan, pair, tp, tg, bl)
+    ncomp = cnt.shape[0]
+    heads = bl.shape[0] // ncomp
+    b = []
+    for n in range(ncomp):
+        hs = pl.ds(n * heads, heads)
+        b.append(bias_gather_steps(plan, bl.at[hs], zb.at[:, hs], bias.at[hs]))
+
+    def both(*steps):
+        def go():
+            for step in steps:
+                step()
+
+        return go
+
+    during = {0: both(b[-1][1], c_[0], b[0][2])} if ncomp > 1 else {}
+    first, attend, leaving = forward_parts(
+        plan, rows1, comp, cnt, x, c, g1, sm, outs, bias, wv, vs, pst, psem, fsem, during, c_[2]
+    )
+    run = [p[0], a[0][0], p[1], a[0][1]]
+    for more in a[1:]:
+        run += [more[0]]
+    run += p[2:]
+    for more in a[1:]:
+        run += [more[1]]
+    run += [b[0][0]]
+    for i in range(2, len(a[0]) - 1):
+        run += [more[i] for more in a]
+    if ncomp > 1:
+        run += [b[0][1], b[1][0]] + [b_ for more in b[1:-1] for b_ in more[1:]]
+        run += [more[-1] for more in a] + [first, b[0][3], b[-1][2], c_[1], b[-1][3], b[0][4], b[-1][4]]
+    else:
+        run += [b[0][1], c_[0]] + [more[-1] for more in a] + [first, b[0][2], c_[1]] + b[0][3:]
+    for step in run + [attend] + c_[3:] + [leaving]:
+        step()
+    plan.finish()
+
+
+def run_gather(ndp, nfs, spots, ws, small, more, size1, size2, d, heads, rows1):
+    sds = jax.ShapeDtypeStruct
+    count = 80 * max(ndp // 4, 2)
+    outs = [sds((nfs, size1, d), BF), sds((nfs, size2, d), BF)]
+    specs = [ANYWHERE] * 2
+    scratch = [pltpu.VMEM((size1, d), BF), pltpu.VMEM((size2, d), BF)]
+    sems = [DMA((count,)), DMA((count,)), DMA((len(ws) + 8,))]
+    ins = list(ws) + list(small)
+    in_specs = [VMEM] * len(ins)
+    if more is not None:
+        pair, tp, comp, cnt, x, c = more
+        ncomp, r, cw, _ = pair.shape
+        nh, rows, full = ncomp * heads, r * ndp, cw * nfs
+        t, dc = c.shape
+        ins += more
+        in_specs += [VMEM, VMEM, SMEM, SMEM, VMEM, VMEM]
+        kept = [(t, d)] * 6 + [(t, dc)] + [(t, d)] * 2
+        outs += [sds((nfs,) + tp.shape, BF), sds((8, d), F32)] + [sds(k, BF) for k in kept]
+        outs += [sds((comp.shape[0], heads, rows, rows), BF)]
+        specs += [VMEM, VMEM] + [ANYWHERE] * (len(kept) + 1)
+        scratch += [pltpu.VMEM((nh, r, cw), BF), pltpu.VMEM((nfs, nh, r, cw), BF), pltpu.VMEM((nh, rows, full), BF),
+                    pltpu.VMEM((nfs, size1, d), BF), pltpu.VMEM((2, heads // 2, rows, rows), BF)]
+        scratch += [pltpu.VMEM(k, BF) for k in kept]
+        sems += [DMA((2,)), DMA((len(kept),))]
     return pl.pallas_call(
-        outer_kernel,
-        grid=(k // kb, n // nb),
-        in_specs=[
-            pl.BlockSpec((t, kb), lambda i, j: (0, i)),
-            pl.BlockSpec((t, nb), lambda i, j: (0, j)),
-        ],
-        out_specs=pl.BlockSpec((kb, nb), lambda i, j: (i, j)),
-        out_shape=jax.ShapeDtypeStruct((k, n), BF),
-        compiler_params=params(60),
-        cost_estimate=cost(2 * t * k * n, 2 * (t * k + t * n + k * n)),
-        name="outer",
-    )(a, b)
-
-
-def split_rows(w, z):
-    return w.reshape(z, w.shape[0] // z, w.shape[1])
+        functools.partial(gather_kernel, ndp, nfs, spots, rows1, more is not None),
+        in_specs=in_specs,
+        out_specs=specs,
+        out_shape=outs,
+        scratch_shapes=scratch + sems,
+        compiler_params=params(61, collective_id=0, has_side_effects=True),
+        name="gather",
+    )(*ins)
+
+
+class Tiles:
+    def __init__(self, bufs, sems):
+        self.bufs, self.sems = bufs, sems
+        self.held = [None] * bufs.shape[0]
+        self.copies = [None] * bufs.shape[0]
+        self.used = [-1] * bufs.shape[0]
+
+    def fetch(self, key, ref, col, width, now):
+        if key in self.held:
+            i = self.held.index(key)
+            self.used[i] = now
+            return i
+        i = self.used.index(min(self.used))
+        self.held[i], self.used[i] = key, now
+        src = ref if width == ref.shape[1] else ref.at[:, pl.ds(col, width)]
+        self.copies[i] = pltpu.make_async_copy(src, self.bufs.at[i, :, pl.ds(0, width)], self.sems.at[i])
+        self.copies[i].start()
+        return i
+
+    def wait(self, i):
+        if self.copies[i] is not None:
+            self.copies[i].wait()
+            self.copies[i] = None
+
+
+def attend_back_phase(comp, p, ops_hbm, outs_hbm, db, during):
+    copies, heads, rows, _ = p.shape
+    t, d = ops_hbm[0].shape
+    ncomp = db.shape[0]
+    groups = 2
+    per, dg, hs = heads // groups, d // groups, d // heads
+    width = min(256, dg)
+    scale = hs ** (-0.5)
+
+    def run(ops, res, pb, dbs, isem, psem, dsem, rsem):
+        inds = [[jnp.full((1, rows), jnp.where(comp[c] == n, 1.0, 0.0), F32).astype(BF) for n in range(ncomp)] for c in range(copies)]
+        for g in range(groups):
+            cols = pl.ds(g * dg, dg)
+            loads = [pltpu.make_async_copy(a.at[:, cols], ops.at[i], isem.at[i]) for i, a in enumerate(ops_hbm)]
+            start(loads)
+
+            def fetch(j, slot):
+                return pltpu.make_async_copy(p.at[:, g * per + j], pb.at[slot], psem.at[slot])
+
+            def flight(j):
+                return pltpu.make_async_copy(dbs.at[j % 2], db.at[:, g * per + j], dsem.at[j % 2])
+
+            fetch(0, 0).start()
+            for c in loads:
+                c.wait()
+            res[...] = jnp.zeros_like(res)
+
+            def one(j, carry):
+                slot = j % 2
+                fetch(j, slot).wait()
+
+                @pl.when(j + 1 < per)
+                def _():
+                    fetch(j + 1, 1 - slot).start()
+
+                @pl.when(j >= 2)
+                def _():
+                    flight(j - 2).wait()
+
+                w = jnp.minimum(j * hs // 128 * 128, dg - width)
+                m = lane_mask(j * hs - w, hs, width)
+                win = pl.ds(pl.multiple_of(w, 128), width)
+                acc = [None] * ncomp
+                for c in range(copies):
+                    rs = pl.ds(c * rows, rows)
+                    dam = ops[3, rs, win] * m
+                    delta = jnp.sum(dam.astype(F32) * ops[4, rs, win].astype(F32), axis=-1, keepdims=True)
+                    pj = pb[slot, c]
+                    ds = (pj.astype(F32) * (dot_nt(dam, ops[2, rs, win]) - delta)).astype(BF)
+                    res[2, rs, win] += dot_tn(pj, dam).astype(BF)
+                    res[0, rs, win] += (dot(ds, ops[1, rs, win] * m) * scale).astype(BF)
+                    res[1, rs, win] += (dot_tn(ds, ops[0, rs, win] * m) * scale).astype(BF)
+                    for n in range(ncomp):
+                        term = ds * inds[c][n]
+                        acc[n] = term if acc[n] is None else acc[n] + term
+                for n in range(ncomp):
+                    dbs[slot, n] = acc[n]
+                flight(j).start()
+                for jj in range(per):
+                    if (g, jj) in during:
+                        pl.when(j == jj)(during[(g, jj)])
+                return carry
+
+            lax.fori_loop(0, per, one, 0)
+            back = [pltpu.make_async_copy(res.at[i], o.at[:, cols], rsem.at[i]) for i, o in enumerate(outs_hbm)]
+            start(back)
+            for c in back + [flight(per - 2), flight(per - 1)]:
+                c.wait()
+
+    pl.run_scoped(
+        run, pltpu.VMEM((5, t, dg), BF), pltpu.VMEM((3, t, dg), BF), pltpu.VMEM((2, copies, rows, rows), BF),
+        pltpu.VMEM((2, ncomp, rows, rows), BF), DMA((5,)), DMA((2,)), DMA((2,)), DMA((3,)),
+    )
+
+
+def last_phase(rows_hbm, c, gm, dcp, g1, sm, vec, outs_hbm, tb, during):
+    t, d = rows_hbm[0].shape
+    dc = c.shape[1]
+    nfs = g1.shape[0]
+    dz, cz = d // nfs, dc // nfs
+    count = t // tb
+
+    def run(wv, b6, cb, gmb, dcb, sgb, cgb, gsb, wsem, isem, osem):
+        load = pltpu.make_async_copy(g1, wv, wsem.at[0])
+        load.start()
+
+        def come(i):
+            at, k = pl.ds(pl.multiple_of(i * tb, tb), tb), i % 2
+            pairs = [(r_.at[at, :], b6.at[k, n]) for n, r_ in enumerate(rows_hbm)]
+            pairs += [(c.at[at, :], cb.at[k]), (gm.at[at, :], gmb.at[k]), (dcp.at[at, :], dcb.at[k])]
+            return [pltpu.make_async_copy(a, b_, isem.at[k, n]) for n, (a, b_) in enumerate(pairs)]
+
+        def leave(i):
+            at, k = pl.ds(pl.multiple_of(i * tb, tb), tb), i % 2
+            bufs = [sgb.at[k], cgb.at[k], gsb.at[k, 0], gsb.at[k, 1]]
+            return [pltpu.make_async_copy(b_, o.at[at, :], osem.at[k, n]) for n, (b_, o) in enumerate(zip(bufs, outs_hbm))]
+
+        start(come(0))
+        vec[...] = jnp.zeros_like(vec)
+        load.wait()
+        ws = [wv.at[:, pl.ds(j * dz, dz), :] for j in range(4)]
+        ws += [wv.at[:, pl.ds(4 * dz + j * cz, cz), :] for j in range(2)]
+
+        def one(i, carry):
+            k = i % 2
+            for c_ in come(i):
+                c_.wait()
+
+            @pl.when(i + 1 < count)
+            def _():
+                start(come(i + 1))
+
+            @pl.when(i >= 2)
+            def _():
+                for c_ in leave(i - 2):
+                    c_.wait()
+
+            r6 = [b6.at[k, n] for n in range(6)]
+            last_body(*r6[:5], cb.at[k], r6[5], gmb.at[k], dcb.at[k], *ws, sm, sgb.at[k], cgb.at[k], gsb.at[k, 0],
+                      gsb.at[k, 1], vec)
+            start(leave(i))
+            for ii in range(count):
+                if ii in during:
+                    pl.when(i == ii)(during[ii])
+            return carry
+
+        lax.fori_loop(0, count, one, 0)
+        for i in range(max(count - 2, 0), count):
+            for c_ in leave(i):
+                c_.wait()
+
+    pl.run_scoped(
+        run, pltpu.VMEM(g1.shape, BF), pltpu.VMEM((2, 6, tb, d), BF), pltpu.VMEM((2, tb, dc), BF),
+        pltpu.VMEM((2, tb, d), F32), pltpu.VMEM((2, tb, dc), F32), pltpu.VMEM((2, tb, d), F32), pltpu.VMEM((2, tb, dc), F32),
+        pltpu.VMEM((2, 2, tb, d), BF), DMA((1,)), DMA((2, 9)), DMA((2, 4)),
+    )
+
+
+def cuts(size, unit):
+    if size % (2 * unit) == 0:
+        return [(0, size // 2), (size // 2, size // 2)]
+    return [(0, size)]
+
+
+ROWS = 384
+LAST = 128
+ORDERS = (
+    "jjjjjSjjSjjjjT",
+    {(0, 1): "T", (0, 5): "S", (1, 2): "S", (1, 6): "T"},
+    {0: "b", 1: "c", 2: "T", 3: "S", 6: "b", 7: "T"},
+    "ScjjjQbjQTjSjRc",
+    "RSTQbRQcRtSTQRtttQRtSTQRSTQRSTQRSTQR",
+)
+
+
+def products_phase(jobs, ins, packs, order, step, state):
+    t, d = ins[0].shape[0], packs[0].shape[2]
+    nz = packs[0].shape[0]
+
+    def run(tiles, outs, tsem, osem):
+        held = Tiles(tiles, tsem)
+        flying = [[] for _ in range(outs.shape[0])]
+        ready = {}
+
+        def operands(j):
+            (li, lc, lw), (ri, rc, rw), _, _ = jobs[j]
+            return (
+                held.fetch((li, lc), ins[li], lc, lw, 2 * j),
+                held.fetch((ri, rc), ins[ri], rc, rw, 2 * j + 1),
+            )
+
+        def job(j):
+            if j not in ready:
+                ready[j] = operands(j)
+            (_, _, lw), _, which, (z0, count, (zr, at)) = jobs[j]
+            li, ri = ready[j]
+            held.wait(li)
+            held.wait(ri)
+            if j + 1 < len(jobs):
+                ready[j + 1] = operands(j + 1)
+            o = j % outs.shape[0]
+            for c in flying[o]:
+                c.wait()
+            kb = min(lw, ROWS)
+
+            def some(i, carry):
+                cols = pl.ds(pl.multiple_of(i * kb, kb), kb)
+                outs[o, cols, :] = dot_tn(tiles[li, :, cols], tiles[ri]).astype(BF)
+                return carry
+
+            lax.fori_loop(0, lw // kb, some, 0)
+            flying[o] = [
+                pltpu.make_async_copy(
+                    outs.at[o, pl.ds(i * zr, zr), :], packs[which].at[z0 + i, pl.ds(at, zr), :], osem.at[o, i]
+                )
+                for i in range(count)
+            ]
+            start(flying[o])
+
+        def settle():
+            for o in range(outs.shape[0]):
+                for c in flying[o]:
+                    c.wait()
+                flying[o] = []
+
+        state["settle"] = settle
+        j = 0
+        for ch in order:
+            if ch == "j":
+                job(j)
+                j += 1
+            else:
+                step(ch)
+        settle()
+        state["settle"] = lambda: None
+
+    pl.run_scoped(run, pltpu.VMEM((4, t, d), BF), pltpu.VMEM((2, d, d), BF), DMA((4,)), DMA((2, nz)))
+
+
+def products_kernel(ndp, nfs, jobs, split, orders, nin, small_at, cuts1, cuts2, full, *refs):
+    ins, rest = list(refs[:nin]), list(refs[nin:])
+
+    def take(n):
+        out = rest[:n]
+        del rest[:n]
+        return out
+
+    if full:
+        p, q, k, v, da, att, x, c, sp, gm, dcp, g1, sm, vec_a, comp, pair, tg = take(17)
+    else:
+        (small,) = take(1)
+    r1, r2, pg1, pg2 = take(4)
+    if full:
+        dq, dk, dv, gsc, gsh, db, sg, cg, pgrad, tiny_out = take(10)
+    per = 5
+    bufs1 = [take(per) for _ in cuts1]
+    bufs2 = [take(per) for _ in cuts2]
+    send, recv, local = take(3)
+    if full:
+        small, vec = take(2)
+        ins += [dq, dk, dv, gsc, gsh]
+    plan = Plan(ndp, nfs, send, recv, local)
+    state = {"settle": lambda: None}
+    lsmall = plan.here(small, pg1.at[:, pl.ds(small_at, 16), :])
+
+    def settle():
+        state["settle"]()
+
+    def settle_small():
+        settle()
+        if full:
+            both = jnp.concatenate([vec_a[...] + vec[...], jnp.zeros_like(vec)], axis=0).astype(BF)
+            d, dc = x.shape[1], c.shape[1]
+            dz, cz = d // nfs, dc // nfs
+            row = lax.broadcasted_iota(jnp.int32, (16, 1), 0)
+            small[...] = jnp.zeros_like(small)
+            for z in range(nfs):
+                wide = dot(both, place(dz, d, z * dz, False))
+                thin = dot(both[:, :dc], place(dz, dc, z * cz, False))
+                small[z, :, 0:dz] = jnp.where((row == 5) | (row == 6), thin, wide).astype(BF)
+        lsmall.start()
+        lsmall.wait()
+
+    def chunks(pg, out, bufs, spans, last):
+        done = []
+        for i, (buf, span) in enumerate(zip(bufs, spans)):
+            at = pl.ds(*span)
+            done.append(reduce_steps(plan, pg.at[:, at], out.at[at], *buf, last if i == len(bufs) - 1 else settle))
+        return done
+
+    lists = {"STU"[i]: steps for i, steps in enumerate(chunks(pg2, r2, bufs2, cuts2, settle))}
+    lists.update({"QR"[i]: steps for i, steps in enumerate(chunks(pg1, r1, bufs1, cuts1, settle_small))})
+    if full:
+        (ob,) = take(1)
+        ncomp = db.shape[0]
+        heads = ob.shape[0] // ncomp
+        for n in range(ncomp):
+            lists["bc"[n]] = bias_reduce_steps(plan, db.at[n], ob.at[pl.ds(n * heads, heads)], *take(5))
+        tacc, tr, tz = take(3)
+        lists["t"] = tiny_steps(plan, tacc, tr, tz, tiny_out, lambda: pair_back(pair, tg, ob, pgrad, tacc))
+    left = {name: list(steps) for name, steps in lists.items()}
+
+    def step(ch):
+        if left.get(ch):
+            left[ch].pop(0)()
+
+    def steps_of(table):
+        return {key: (lambda chs: lambda: [step(ch) for ch in chs] and None)(chs) for key, chs in table.items()}
+
+    first, in_attend, in_last, second, tail = orders
+    plan.barrier()
+    products_phase(jobs[:split], ins, (pg1, pg2), first, step, state)
+    if full:
+        attend_back_phase(comp, p, (q, k, v, da, att), (dq, dk, dv), db, steps_of(in_attend))
+        step("b")
+        step("c")
+        last_phase((dq, dk, dv, ins[14], x, sp), c, gm, dcp, g1, sm, vec, (sg, cg, gsc, gsh), LAST, steps_of(in_last))
+    products_phase(jobs[split:], ins, (pg1, pg2), second, step, state)
+    for ch in tail:
+        step(ch)
+    for name in left:
+        while left[name]:
+            step(name)
+    plan.finish()
+
+
+def run_products(ndp, nfs, jobs, split, orders, ins, more, small, small_at, size1, size2):
+    t = ins[0].shape[0]
+    d = ins[1].shape[1]
+    nchip = ndp // 2
+    sds = jax.ShapeDtypeStruct
+
+    def sums(*shape):
+        return [pltpu.VMEM((nchip,) + shape, BF), pltpu.VMEM((nchip,) + shape, BF), pltpu.VMEM((max(nchip - 1, 1),) + shape, BF)]
+
+    cuts1, cuts2 = cuts(size1, 16 * ndp), cuts(size2, 16 * ndp)
+
+    def scratch(spans):
+        got = []
+        for _, size in spans:
+            n = size // ndp
+            got += sums(nfs, n, d) + [pltpu.VMEM((nfs - 1, n, d), BF), pltpu.VMEM((n, d), BF)]
+        return got
+
+    count = 100 * max(ndp // 4, 2)
+    outs = [sds((size1, d), BF), sds((size2, d), BF), sds((nfs, size1, d), BF), sds((nfs, size2, d), BF)]
+    out_specs = [ANYWHERE] * 4
+    in_specs = [ANYWHERE] * len(ins)
+    tail_scratch = []
+    if more is not None:
+        p, pair, dc = more[0], more[15], more[7].shape[1]
+        _, heads, rows, full = p.shape
+        ncomp, r, cw, width = pair.shape
+        levels = len(bits_of(ndp))
+        in_specs += [ANYWHERE] * 12 + [VMEM, VMEM, SMEM, ANYWHERE, VMEM]
+        extra = list(more)
+        outs += [sds((t, d), BF)] * 5 + [sds((ncomp, heads, rows, full), BF), sds((t, d), F32), sds((t, dc), F32),
+                                         sds(pair.shape, F32), sds((32, width), F32)]
+        out_specs += [ANYWHERE] * 9 + [VMEM]
+        tail_scratch = [pltpu.VMEM((nfs, 16, d), BF), pltpu.VMEM((8, d), F32), pltpu.VMEM((ncomp * heads, r, cw), F32)]
+        tail_scratch += (sums(heads, r, full) + [pltpu.VMEM((nfs, heads, r, cw), BF), pltpu.VMEM((nfs - 1, heads, r, cw), BF)]) * ncomp
+        tail_scratch += [pltpu.VMEM((k, 32, width), F32) for k in (levels + 1, levels, nfs - 1)]
+    else:
+        in_specs += [VMEM]
+        extra = [small]
+    return pl.pallas_call(
+        functools.partial(products_kernel, ndp, nfs, jobs, split, orders, len(ins), small_at, cuts1, cuts2,
+                          more is not None),
+        in_specs=in_specs,
+        out_specs=out_specs,
+        out_shape=outs,
+        scratch_shapes=scratch(cuts1) + scratch(cuts2)
+        + [DMA((count,)), DMA((count,)), DMA((8 * nchip + 10,))] + tail_scratch,
+        compiler_params=params(62, collective_id=1, has_side_effects=True),
+        name="products",
+    )(*ins, *extra)
+
+
+def emit_kernel(spots, r1, r2, *outs):
+    for o, (which, at) in zip(outs, spots):
+        r = (r1, r2)[which]
+        n = o.shape[0]
+        for i, row in enumerate(at):
+            w = r.shape[1]
+            o[:, i * w : i * w + w] = r[row : row + n, :].astype(F32)
+
+
+def run_emit(r1, r2, spots, shapes):
+    sds = jax.ShapeDtypeStruct
+    return pl.pallas_call(
+        functools.partial(emit_kernel, spots),
+        in_specs=[VMEM] * 2,
+        out_specs=[VMEM] * len(shapes),
+        out_shape=[sds(k, F32) for k in shapes],
+        compiler_params=params(40),
+        name="emit",
+    )(r1, r2)
 
 
 def body(ndp, nfs, *args):
@@ -465,113 +1502,128 @@
     x = single.reshape(t, d)
     c = condition.reshape(t, dc)
     ct = cotangent.reshape(t, d)
-    me = lax.axis_index(DP)
     unit = 16 * ndp
 
     def padded(total):
         return -(-total // unit) * unit
 
-    def row(v):
-        return jnp.pad(v, (0, d - v.shape[0]))[None, :]
-
     vectors = (scale_bias, query_bias, branch_gate_bias, transition_scale_bias, final_gate_bias,
                condition_gain, transition_gain)
-    small = jnp.concatenate([row(v) for v in vectors] + [jnp.zeros((1, d), BF)], axis=0)
-    rows1 = 4 * dz + 2 * scale_weight.shape[0]
-    pack1 = jnp.concatenate(
-        [query_weight, key_weight, value_weight, gate_weight, scale_weight, shift_weight, small], axis=0
+    small = [v[None, :] for v in vectors]
+    cz, fz = dc // nfs, hidden_output.shape[0]
+    rows1 = 4 * dz + 2 * cz
+    rows2 = fz + 5 * dz + 4 * cz
+    size1, size2 = padded(rows1 + 16), padded(rows2)
+    ws, spots = [], []
+
+    def spot(w, which, at, col=0):
+        ws.append(w)
+        spots.append((which, col, d, at))
+
+    for i, w in enumerate((query_weight, key_weight, value_weight, gate_weight)):
+        spot(w, 0, i * dz)
+    spot(scale_weight, 0, 4 * dz)
+    spot(shift_weight, 0, 4 * dz + cz)
+    spot(hidden_output, 1, 0)
+    spot(output_weight, 1, fz)
+    for i, (w, col) in enumerate(((hidden_gate, 0), (hidden_gate, d), (hidden_value, 0), (hidden_value, d))):
+        spot(w, 1, fz + (i + 1) * dz, col)
+    for i, w in enumerate((branch_gate_weight, transition_scale_weight, transition_shift_weight, final_gate_weight)):
+        spot(w, 1, fz + 5 * dz + i * cz)
+    pair_width = pair_weight.shape[0] * nfs
+    local_rows, local_cols = pair_tensor.shape[1:3]
+    pgw = jnp.concatenate([pair_weight, pair_gain[:, None]], axis=1)
+    aligned = local_rows % 16 == 0 and heads == 16 and pair_width == 128
+    if aligned:
+        tp = jnp.pad(pgw, ((0, 0), (0, pair_width - heads - 1)))
+        more = [pair_tensor, tp, complex_of, counts, x, c]
+        g1, g2, tg, sm, first_in, q, k, v, gp, sp, cl1, att, gated, p = run_gather(
+            ndp, nfs, tuple(spots), ws, small, more, size1, size2, d, heads, rows1
+        )
+    else:
+        pgw = lax.all_gather(pgw, FS, axis=0, tiled=True)
+        pw, pgain = pgw[:, :heads], pgw[:, heads].astype(F32)
+        pair_norm, pair_rstd = norm(pair_tensor.astype(F32))
+        pair_low = (pair_norm * pgain).astype(BF)
+        bias_local = jnp.transpose(dot(pair_low, pw).astype(BF), (0, 3, 1, 2))
+        g1, g2 = run_gather(ndp, nfs, tuple(spots), ws, small, None, size1, size2, d, heads, rows1)
+        bias = lax.all_gather(bias_local, FS, axis=3, tiled=True)
+        bias = lax.all_gather(bias, DP, axis=2, tiled=True)
+        tg = None
+        sm = jnp.transpose(g1[:, rows1 : rows1 + 8, :dz], (1, 0, 2)).reshape(8, d).astype(F32)
+        gains = g1[:, rows1 + 5, : 2 * cz].reshape(nfs, 2, cz)
+        gains = jnp.transpose(gains, (1, 0, 2)).reshape(2, dc).astype(F32)
+        sm = jnp.concatenate([sm[:5], jnp.pad(gains, ((0, 0), (0, d - dc))), sm[7:]], axis=0)
+        first_in, q, k, v, gp, sp, cl1 = run_first(x, c, g1, sm, rows)
+        p, att, gated = run_attend(complex_of, counts, q, k, v, gp, bias, 2)
+
+    (out, gm, dcp, si, act, cl2, gt2, gz2, gh, gv, gsc2, gsh2, gt1, gz1, da, dg, vec_a) = run_middle(
+        complex_of, counts, x, c, ct, gated, att, gp, g2, sm, rows
     )
-    size1 = padded(rows1 + 8)
-    pack1 = jnp.pad(pack1, ((0, size1 - pack1.shape[0]), (0, 0)))
-    pack2 = jnp.concatenate(
-        [hidden_output, output_weight, hidden_gate[:, :d], hidden_gate[:, d:], hidden_value[:, :d],
-         hidden_value[:, d:], branch_gate_weight, transition_scale_weight, transition_shift_weight,
-         final_gate_weight], axis=0
-    )
-    rows2 = pack2.shape[0]
-    size2 = padded(rows2)
-    pack2 = jnp.pad(pack2, ((0, size2 - rows2), (0, 0)))
-
-    def gather(pack):
-        n = pack.shape[0] // ndp
-        mine = lax.dynamic_slice_in_dim(pack, me * n, n, axis=0)
-        return lax.all_gather(mine, (FS, DP), axis=0, tiled=True).reshape(nfs, pack.shape[0], d)
-
-    g1 = gather(pack1)
-    g2 = gather(pack2)
-    pgain = lax.all_gather(pair_gain, FS, axis=0, tiled=True).astype(F32)
-    pw = lax.all_gather(pair_weight, FS, axis=0, tiled=True)
-    sm = jnp.transpose(g1[:, rows1 : rows1 + 8, :dz], (1, 0, 2)).reshape(8, d).astype(F32)
-    cz = dc // nfs
-    gains = jnp.transpose(g1[:, rows1 + 5 : rows1 + 7, :cz], (1, 0, 2)).reshape(2, dc).astype(F32)
-    sm = jnp.concatenate([sm[:5], jnp.pad(gains, ((0, 0), (0, d - dc))), sm[7:]], axis=0)
-
-    pair_float = pair_tensor.astype(F32)
-    pair_norm, pair_rstd = norm(pair_float)
-    pair_low = (pair_norm * pgain).astype(BF)
-    bias_local = jnp.transpose(dot(pair_low, pw).astype(BF), (0, 3, 1, 2))
-    bias = lax.all_gather(bias_local, FS, axis=3, tiled=True)
-    bias = lax.all_gather(bias, DP, axis=2, tiled=True)
-
-    first_in, q, k, v, gp, sp, cl1 = run_first(x, c, g1, sm, rows)
-    p, att, gated = run_attend(complex_of, counts, q, k, v, gp, bias, 2)
-    (out, gm, dcp, si, act, cl2, gt2, gz2, gh, gv, gsc2, gsh2, gt1, gz1, da, dg, vec_a) = run_middle(
-        complex_of, counts, x, c, ct, gated, att, gp, g2, sm, rows // 2
-    )
-    dq, dk, dv, db = run_attend_back(complex_of, p, q, k, v, da, att, ncomp, 2)
-    sgrad, cgrad, gsc1, gsh1, vec_b = run_last(dq, dk, dv, dg, x, c, sp, gm, dcp, g1, sm, rows)
-
-    w_hg = outer(si, gh)
-    w_hv = outer(si, gv)
-    grads2 = [outer(act, gt2), outer(gated, gt1), w_hg[:, :d], w_hg[:, d:], w_hv[:, :d], w_hv[:, d:],
-              outer(c, gz1), outer(cl2, gsc2), outer(cl2, gsh2), outer(c, gz2)]
-    pg2 = jnp.concatenate([split_rows(w, nfs) for w in grads2], axis=1)
-    pg2 = jnp.pad(pg2, ((0, 0), (0, size2 - rows2), (0, 0)))
-
-    def reduce(pack):
-        n = pack.shape[1] // ndp
-        part_sum = lax.psum_scatter(
-            pack.reshape(nfs * pack.shape[1], d), (FS, DP), scatter_dimension=0, tiled=True
+    small_grad = None
+    if not aligned:
+        dq, dk, dv, db = run_attend_back(complex_of, p, q, k, v, da, att, ncomp, 2)
+        sgrad, cgrad, gsc1, gsh1, vec_b = run_last(dq, dk, dv, dg, x, c, sp, gm, dcp, g1, sm, rows)
+        vec = (vec_a + vec_b).astype(BF)
+        vz = jnp.transpose(vec.reshape(8, nfs, dz), (1, 0, 2))
+        cv = jnp.transpose(vec[5:7, :dc].reshape(2, nfs, cz), (1, 0, 2))
+        vz = jnp.concatenate(
+            [vz[:, :5], jnp.pad(cv, ((0, 0), (0, 0), (0, dz - cz))), jnp.zeros((nfs, 9, dz), BF)], axis=1
         )
-        return lax.all_gather(part_sum, DP, axis=0, tiled=True).astype(F32)
-
-    r2 = reduce(pg2)
-
-    partial_rows = lax.psum_scatter(db, DP, scatter_dimension=2, tiled=True)
-    bias_grad = lax.psum_scatter(partial_rows, FS, scatter_dimension=3, tiled=True)
-    bias_grad = jnp.transpose(bias_grad, (0, 2, 3, 1))
-    pair_width = pair_low.shape[3]
-    pw_grad = dot_tn(pair_low.reshape(-1, pair_width), bias_grad.reshape(-1, heads))
-    grad_low = dot(bias_grad, pw.T)
-    pgain_grad = jnp.sum(grad_low * pair_norm, axis=(0, 1, 2))
-    pair_grad = norm_back(pair_norm, pair_rstd, grad_low * pgain)
-
-    vec = (vec_a + vec_b).astype(BF)
-    vz = jnp.transpose(vec.reshape(8, nfs, dz), (1, 0, 2))
-    cv = jnp.transpose(vec[5:7, :dc].reshape(2, nfs, cz), (1, 0, 2))
-    vz = jnp.concatenate(
-        [vz[:, :5], jnp.pad(cv, ((0, 0), (0, 0), (0, dz - cz))), jnp.zeros((nfs, 1, dz), BF)], axis=1
-    )
-    small_grad = jnp.pad(vz, ((0, 0), (0, 0), (0, d - dz)))
-    pgz = jnp.pad(pgain_grad.astype(BF).reshape(nfs, 1, -1), ((0, 0), (0, 0), (0, d - pair_width // nfs)))
-    pwz = jnp.pad(pw_grad.astype(BF).reshape(nfs, 1, -1), ((0, 0), (0, 0), (0, d - pair_width * heads // nfs)))
-    grads1 = [outer(first_in, dq), outer(first_in, dk), outer(first_in, dv), outer(first_in, dg),
-              outer(cl1, gsc1), outer(cl1, gsh1)]
-    pg1 = jnp.concatenate([split_rows(w, nfs) for w in grads1] + [small_grad, pgz, pwz], axis=1)
-    pg1 = jnp.pad(pg1, ((0, 0), (0, size1 - pg1.shape[1]), (0, 0)))
-    r1 = reduce(pg1)
-
-    def take(r, at, n):
-        return r[at : at + n]
-
-    fz = hidden_output.shape[0]
-    o1 = [take(r1, i * dz, dz) for i in range(4)]
-    s1 = [take(r1, 4 * dz + i * cz, cz) for i in range(2)]
-    sv = r1[rows1 : rows1 + 8]
-    ext = r1[rows1 + 8 : rows1 + 10]
+        small_grad = jnp.pad(vz, ((0, 0), (0, 0), (0, d - dz)))
+    ins = [act, gt2, si, gh, gv, gated, gt1, c, gz1, gz2, cl2, gsc2, gsh2, first_in, dg, cl1]
+    hz = nfs // 2
+
+    def job(li, lc, lw, ri, rc, which, at):
+        if lw == dc:
+            where = (0, nfs, (cz, at))
+        elif li == 0:
+            where = (lc // d * hz, hz, (fz, at))
+        else:
+            where = (0, nfs, (dz, at))
+        return ((li, lc, lw), (ri, rc, d), which, where)
+
+    c0 = fz + 5 * dz
+    jobs = [
+        job(0, 0, d, 1, 0, 1, 0), job(0, d, d, 1, 0, 1, 0),
+        job(2, 0, d, 3, 0, 1, fz + dz), job(2, 0, d, 3, d, 1, fz + 2 * dz),
+        job(5, 0, d, 6, 0, 1, fz),
+        job(2, 0, d, 4, 0, 1, fz + 3 * dz), job(2, 0, d, 4, d, 1, fz + 4 * dz),
+        job(7, 0, dc, 8, 0, 1, c0), job(7, 0, dc, 9, 0, 1, c0 + 3 * cz),
+        job(10, 0, dc, 11, 0, 1, c0 + cz), job(10, 0, dc, 12, 0, 1, c0 + 2 * cz),
+        job(13, 0, d, 16, 0, 0, 0), job(13, 0, d, 17, 0, 0, dz), job(13, 0, d, 18, 0, 0, 2 * dz),
+        job(13, 0, d, 14, 0, 0, 3 * dz),
+        job(15, 0, dc, 19, 0, 0, 4 * dz), job(15, 0, dc, 20, 0, 0, 4 * dz + cz),
+    ]
+    if aligned:
+        more = [p, q, k, v, da, att, x, c, sp, gm, dcp, g1, sm, vec_a, complex_of, pair_tensor, tg]
+    else:
+        more = None
+        ins += [dq, dk, dv, gsc1, gsh1]
+    moved = run_products(ndp, nfs, jobs, 11, ORDERS, ins, more, small_grad, rows1, size1, size2)
+    r1, r2 = moved[:2]
+    pz = pair_width // nfs
+    if aligned:
+        sgrad, cgrad, pair_grad = moved[10:13]
+        tiny = lax.dynamic_slice_in_dim(moved[13][: heads + 1], lax.axis_index(FS) * pz, pz, axis=1).T
+    else:
+        bias_sum = lax.psum_scatter(db, DP, scatter_dimension=2, tiled=True)
+        bias_sum = lax.psum_scatter(bias_sum, FS, scatter_dimension=3, tiled=True)
+        bias_grad = jnp.transpose(bias_sum, (0, 2, 3, 1))
+        pw_grad = dot_tn(pair_low.reshape(-1, pair_width), bias_grad.reshape(-1, heads))
+        grad_low = dot(bias_grad, pw.T)
+        pgain_grad = jnp.sum(grad_low * pair_norm, axis=(0, 1, 2))
+        pair_grad = norm_back(pair_norm, pair_rstd, grad_low * pgain)
+        tiny = lax.psum(jnp.concatenate([pw_grad, pgain_grad[:, None]], axis=1), (DP, FS))
+        tiny = lax.dynamic_slice_in_dim(tiny, lax.axis_index(FS) * pz, pz, axis=0)
+    sv = r1[rows1 : rows1 + 8].astype(F32)
     at = fz + 5 * dz
-    o2 = [take(r2, fz + i * dz, dz) for i in range(5)]
-    c2 = [take(r2, at + i * cz, cz) for i in range(4)]
+    spots = tuple((0, (i * dz,)) for i in range(4)) + tuple((0, (4 * dz + i * cz,)) for i in range(2))
+    spots += ((1, (fz,)), (1, (fz + dz, fz + 2 * dz)), (1, (fz + 3 * dz, fz + 4 * dz)), (1, (0,)))
+    spots += tuple((1, (at + i * cz,)) for i in range(4))
+    shapes = [(dz, d)] * 4 + [(cz, d)] * 2 + [(dz, d), (dz, 2 * d), (dz, 2 * d), (fz, d)] + [(cz, d)] * 4
+    w = run_emit(r1, r2, spots, shapes)
+    o1, s1, o2, c2 = w[:4], w[4:6], w[6:10], w[10:]
     shape3 = (copies, rows, d)
     return (
         out.reshape(shape3),
@@ -588,17 +1640,17 @@
         o1[2],
         o1[3],
         o2[0],
-        ext[0, : pair_width // nfs],
-        ext[1, : pair_width * heads // nfs].reshape(pair_width // nfs, heads),
+        tiny[:, heads],
+        tiny[:, :heads],
         c2[0],
         sv[2, :dz],
         sv[6, :cz],
         c2[1],
         sv[3, :dz],
         c2[2],
-        jnp.concatenate([o2[1], o2[2]], axis=1),
-        jnp.concatenate([o2[3], o2[4]], axis=1),
-        take(r2, 0, fz),
+        o2[1],
+        o2[2],
+        o2[3],
         c2[3],
         sv[4, :dz],
     )

time: 886 us -> 430 us (0.49)
  waiting for transfers between devices: 474 us -> 0 us
  Pallas kernels: 202 us -> 399 us
  local copies, waits for them, and re-layouts: 124 us -> 20.7 us
  other arithmetic: 22.7 us -> 1.39 us
  blocking collectives: 21 us -> 0 us
  matrix products: 18.9 us -> 0 us
  between operations: 15.8 us -> 1.15 us
    all_gather x6 -> x0, waiting for transfers between devices: 276 us -> none  [the longest x2 135 us: gather(): lax.all_gather(mine, (FS, DP), axis=0, tiled=True)]
    pallas_call x18 -> x3, Pallas kernels: 154 us -> 357 us  [the longest x1 197 us: run_products(): pl.pallas_call(functools.partial(products_kernel, ndp, nfs, jobs, split,...]
    reduce_scatter x3 -> x0, waiting for transfers between devices: 198 us -> none  [the longest x2 151 us: reduce(): lax.psum_scatter(pack.reshape(nfs * pack.shape[1], d), (FS, DP), scatter_...]
    concatenate x5 -> x0, local copies, waits for them, and re-layouts: 48 us -> none  [the longest x1 35.6 us: body(): jnp.concatenate([split_rows(w, nfs) for w in grads1] + [small_grad, pgz,...]
    dot_general x3 -> x0, matrix products: 18.9 us -> none  [the longest x2 13.8 us: dot(): return jnp.dot(a, b, preferred_element_type=F32)]
    unnamed x106 -> x16, local copies, waits for them, and re-layouts: 30 us -> 11.5 us
    pad x12 -> x0, local copies, waits for them, and re-layouts: 17.5 us -> none  [the longest x1 9.72 us: body(): pg2 = jnp.pad(pg2, ((0, 0), (0, size2 - rows2), (0, 0)))]
    mul x1 -> x0, other arithmetic: 11.1 us -> none  [norm_back(): r * (u - jnp.mean(u, axis=-1, keepdims=True) - n * jnp.mean(u * n, axis=-...]
  transfers between devices with their start and end apart: 10 -> 0, of which waited for: 9 -> 0; matrix products, arithmetic and copies ran while one was open for 15% -> 0% of each run, Pallas kernels for 14% -> 0%
where the time goes in v1:
time: 430 us; the launch traced here: 423 us
  Pallas kernels  399 us (93%)
  local copies, waits for them, and re-layouts  20.7 us (5%)
    pallas_call x1, Pallas kernels, run_products(): pl.pallas_call(functools.partial(products_kernel, ndp, nfs, jobs, split,...  197 us
    pallas_call x1, Pallas kernels, run_gather(): pl.pallas_call(functools.partial(gather_kernel, ndp, nfs, spots, rows1, m...  156 us
    pallas_call x1, Pallas kernels, run_middle(): pl.pallas_call(functools.partial(middle_kernel, per_copy), grid_spec=pltp...  42.9 us
    unnamed x16, local copies, waits for them, and re-layouts  11.5 us

profile of v1, /device:TPU:1, one launch (start us, length us, event | category | flops | bytes accessed | tf_op | source)
XLA Modules:
  0.0 422.6 jit_solution(17620540500744271691)
XLA Ops:
  0.7 1.2 broadcast_in_dim.24.refs_16_
  1.9 1.2 broadcast_in_dim.25.refs_17_
  3.1 1.2 broadcast_in_dim.26.refs_18_
  4.3 1.2 broadcast_in_dim.27.refs_19_
  5.5 1.2 broadcast_in_dim.28.refs_20_
  6.8 0.7 copy.57
  7.5 0.8 copy.56
  8.3 0.7 fusion.2.refs_24_
  9.0 155.6 %gather.1 = (bf16[4,1024,768]{2,1,0:T(8,128)(2,1)}, bf16[4,1792,768]{2,1,0:T(8,128)(2,1)}, bf16[4,32,128]{2,1,0:T(8,128)(2,1)}, f32[8,768]{1,0:T(8,128)}, bf16[1...) custom-call(bf16[192,768]{1,0:T(8,128)(2,1)} %refs_0_.1, ...), custom_call_target="tpu_custom_call" | custom-call | tf_op jit(solution)/shard_map/gather/pallas_call | solution.py:1075
  164.6 42.9 %middle.1 = (bf16[1152,768]{1,0:T(8,128)(2,1)}, f32[1152,768]{1,0:T(8,128)}, f32[1152,384]{1,0:T(8,128)}, bf16[1152,768]{1,0:T(8,128)(2,1)}, bf16[1152,1536]{1,0...) custom-call(s32[3]{0:T(128)} %refs_30_.1, s32[2]{0:T(128)} %cnt.1, ...), custom_call_target="tpu_custom_call" | custom-call | flops 24461180928 | bytes 62914560 | tf_op jit(solution)/shard_map/middle/pallas_call | solution.py:362
  207.4 197.3 %products.1 = (bf16[1024,768]{1,0:T(8,128)(2,1)}, bf16[1792,768]{1,0:T(8,128)(2,1)}, bf16[4,1024,768]{2,1,0:T(8,128)(2,1)}, bf16[4,1792,768]{2,1,0:T(8,128)(2,1)...) custom-call(bf16[1152,1536]{1,0:T(8,128)(2,1)} %get-tuple-element.84, ...), custom_call_target="tpu_custom_call" | custom-call | tf_op jit(solution)/shard_map/products/pallas_call | solution.py:1456
  404.8 0.7 slice_convert_fusion
  405.5 0.5 slice_bitcast_fusion
  406.0 0.0 copy-start
  406.0 1.8 copy-done
  407.8 0.0 copy-start.1
  407.8 1.4 copy-done.1
  409.2 0.0 copy-start.3
  409.2 0.0 slice-start
  409.2 3.6 emit.1
  412.8 0.6 fusion.3
  413.4 0.0 copy-done.3
  413.4 0.1 dynamic-slice_bitcast_fusion
  413.5 0.5 slice_bitcast_fusion.1
  414.0 0.6 slice.48
  414.6 0.0 copy-start.2
  414.6 0.0 slice-start.1
  414.6 4.2 copy.61
  418.8 0.0 copy-done.2
  418.8 1.2 copy.62
  420.0 0.0 slice-done
  420.0 0.0 slice-done.1
  420.0 2.2 copy.63
  (2 shorter events, 0.0 us)
Async XLA Ops:
  406.0 1.8 copy-start
  407.8 1.4 copy-start.1
  409.2 4.2 copy-start.3
  409.2 10.8 %slice-start = ((s8[4718592]{0:T(1024)(128)(4,1)}), s8[524288]{0:T(1024)(128)(4,1)S(1)}, s32[]{:S(2)}) async-start(s8[4718592]{0:T(1024)(128)(4,1)} %bitcast.29), calls=%async_computation | async-start | bytes 1048576
  414.6 4.2 copy-start.2
  414.6 5.4 %slice-start.1 = ((s8[4718592]{0:T(1024)(128)(4,1)}), s8[4194304]{0:T(1024)(128)(4,1)S(1)}, s32[]{:S(2)}) async-start(s8[4718592]{0:T(1024)(128)(4,1)} %bitcast.29), calls=%async_computation.1 | async-start | bytes 8388608

commit v2 on v1

--- a/solution.py
+++ b/solution.py
@@ -874,6 +874,9 @@
 SMEM = pl.BlockSpec(memory_space=pltpu.SMEM)
 
 
+WITHIN = 0
+
+
 def fill_vectors(small, s1, rows1):
     parts = [v[...].astype(F32) for v in small]
     v = jnp.concatenate(parts[:5] + [jnp.concatenate(parts[5:], axis=1)], axis=0)
@@ -954,7 +957,7 @@
             attend_body(per, hs, cnt[n], view(q), view(k), view(v), lambda j: bias[n * heads + g * per + j], view(gp),
                         keep, view(att), view(gated))
             flight(it).start()
-            pl.when(it == copies * groups // 2)(within)
+            pl.when(it == WITHIN)(within)
             return carry
 
         lax.fori_loop(0, copies * groups, one, 0)

time: 430 us -> 423 us (0.984)
  Pallas kernels: 399 us -> 392 us
    pallas_call x1, Pallas kernels: 156 us -> 149 us  [run_gather(): pl.pallas_call(functools.partial(gather_kernel, ndp, nfs, spots, rows1, m...]
where the time goes in v2:
time: 423 us; the launch traced here: 416 us
  Pallas kernels  392 us (93%)
  local copies, waits for them, and re-layouts  20.7 us (5%)
    pallas_call x1, Pallas kernels, run_products(): pl.pallas_call(functools.partial(products_kernel, ndp, nfs, jobs, split,...  197 us
    pallas_call x1, Pallas kernels, run_gather(): pl.pallas_call(functools.partial(gather_kernel, ndp, nfs, spots, rows1, m...  149 us
    pallas_call x1, Pallas kernels, run_middle(): pl.pallas_call(functools.partial(middle_kernel, per_copy), grid_spec=pltp...  42.9 us
    unnamed x16, local copies, waits for them, and re-layouts  11.5 us

profile of v2, /device:TPU:1, one launch (start us, length us, event | category | flops | bytes accessed | tf_op | source)
XLA Modules:
  0.0 415.6 jit_solution(995243766500638602)
XLA Ops:
  0.7 1.2 broadcast_in_dim.24.refs_16_
  1.9 1.2 broadcast_in_dim.25.refs_17_
  3.1 1.2 broadcast_in_dim.26.refs_18_
  4.3 1.2 broadcast_in_dim.27.refs_19_
  5.5 1.2 broadcast_in_dim.28.refs_20_
  6.8 0.7 copy.57
  7.5 0.8 copy.56
  8.3 0.7 fusion.2.refs_24_
  9.0 149.2 %gather.1 = (bf16[4,1024,768]{2,1,0:T(8,128)(2,1)}, bf16[4,1792,768]{2,1,0:T(8,128)(2,1)}, bf16[4,32,128]{2,1,0:T(8,128)(2,1)}, f32[8,768]{1,0:T(8,128)}, bf16[1...) custom-call(bf16[192,768]{1,0:T(8,128)(2,1)} %refs_0_.1, ...), custom_call_target="tpu_custom_call" | custom-call | tf_op jit(solution)/shard_map/gather/pallas_call | solution.py:1078
  158.2 42.9 %middle.1 = (bf16[1152,768]{1,0:T(8,128)(2,1)}, f32[1152,768]{1,0:T(8,128)}, f32[1152,384]{1,0:T(8,128)}, bf16[1152,768]{1,0:T(8,128)(2,1)}, bf16[1152,1536]{1,0...) custom-call(s32[3]{0:T(128)} %refs_30_.1, s32[2]{0:T(128)} %cnt.1, ...), custom_call_target="tpu_custom_call" | custom-call | flops 24461180928 | bytes 62914560 | tf_op jit(solution)/shard_map/middle/pallas_call | solution.py:362
  201.0 196.8 %products.1 = (bf16[1024,768]{1,0:T(8,128)(2,1)}, bf16[1792,768]{1,0:T(8,128)(2,1)}, bf16[4,1024,768]{2,1,0:T(8,128)(2,1)}, bf16[4,1792,768]{2,1,0:T(8,128)(2,1)...) custom-call(bf16[1152,1536]{1,0:T(8,128)(2,1)} %get-tuple-element.84, ...), custom_call_target="tpu_custom_call" | custom-call | tf_op jit(solution)/shard_map/products/pallas_call | solution.py:1459
  397.8 0.7 slice_convert_fusion
  398.5 0.5 slice_bitcast_fusion
  399.0 0.0 copy-start
  399.0 1.8 copy-done
  400.8 0.0 copy-start.1
  400.8 1.4 copy-done.1
  402.2 0.0 copy-start.3
  402.2 0.0 slice-start
  402.2 3.6 emit.1
  405.8 0.6 fusion.3
  406.4 0.0 copy-done.3
  406.4 0.1 dynamic-slice_bitcast_fusion
  406.5 0.5 slice_bitcast_fusion.1
  407.0 0.6 slice.48
  407.6 0.0 copy-start.2
  407.6 0.0 slice-start.1
  407.6 4.2 %copy.61 = f32[3,384,768]{2,1,0:T(8,128)} copy(f32[3,384,768]{2,1,0:T(8,128)} %bitcast.31) | data formatting | bytes 7077888
  411.8 0.0 copy-done.2
  411.8 1.2 copy.62
  413.0 0.0 slice-done
  413.0 0.0 slice-done.1
  413.0 2.2 copy.63
  (2 shorter events, 0.0 us)
Async XLA Ops:
  399.0 1.8 copy-start
  400.8 1.4 copy-start.1
  402.2 4.2 %copy-start.3 = (f32[32,128]{1,0:T(8,128)S(1)}, f32[32,128]{1,0:T(8,128)}, u32[]{:S(2)}) copy-start(f32[32,128]{1,0:T(8,128)} %get-tuple-element.121) | copy-start | bytes 49156
  402.2 10.8 %slice-start = ((s8[4718592]{0:T(1024)(128)(4,1)}), s8[524288]{0:T(1024)(128)(4,1)S(1)}, s32[]{:S(2)}) async-start(s8[4718592]{0:T(1024)(128)(4,1)} %bitcast.29), calls=%async_computation | async-start | bytes 1048576
  407.6 4.2 %copy-start.2 = (f32[1152,384]{1,0:T(8,128)S(1)}, f32[1152,384]{1,0:T(8,128)}, u32[]{:S(2)}) copy-start(f32[1152,384]{1,0:T(8,128)} %get-tuple-element.110) | copy-start | bytes 5308420
  407.6 5.4 %slice-start.1 = ((s8[4718592]{0:T(1024)(128)(4,1)}), s8[4194304]{0:T(1024)(128)(4,1)S(1)}, s32[]{:S(2)}) async-start(s8[4718592]{0:T(1024)(128)(4,1)} %bitcast.29), calls=%async_computation.1 | async-start | bytes 8388608
